TPU v7x, 256 devices: a whole 4x4x8 slice. The times are simulated.
256 devices in a mesh: src: 2 (over z_hi), bl: 32 (over x, z_lo, core), ch: 4 (over y).
Axes of the slice: x: 4, y: 4, z: 8 (z_hi: 2, z_lo: 4; z = z_hi * 4 + z_lo), core: 2. Of those that a mesh axis runs over, the one named last changes fastest.
Arguments:
- observed: float32 [2, 16, 16384], P(None, 'ch', 'bl'), may hold values from -6 to 6
- weights: float32 [16, 16384], P('ch', 'bl'), may hold values from 0.3 to 3
- pairs: int32 [2, 16384], P(None, 'bl'), may hold values from 0 to 511
- positions: float32 [512, 2], P('bl'), may hold values from -1 to 1
- centres: float32 [2, 32], replicated, may hold values from -0.6 to 0.6
- assign: int32 [512], P('src'), may hold values from 0 to 31
- amplitude: float32 [512], P('src'), may hold values from 0.01 to 0.1
- offsets: float32 [2, 512], P(None, 'src'), may hold values from -2 to 2
- widths: float32 [512], P('src'), may hold values from 0.02 to 0.1
- block_index: int32 [1], replicated, may hold values from 0 to 511
Outputs:
- grad_comp: float32 [4, 512], P(None, 'src')
- grad_centre: float32 [2, 32], replicated
- residual: float32 [2, 16, 16384], P(None, 'ch', 'bl')
All inputs are finite; a program needn't handle non-finite values.
Results may differ from a plain program's by a relative error of at most 0.0003.
Values sent between devices are 32-bit elements; how exact they have to be, the bound alone decides.
A program may use at most 64 MiB of HBM per device.

v0:
```python
import math

import jax
import jax.numpy as jnp
from jax import lax
from jax.sharding import PartitionSpec as P

BLOCK_CHANNELS = 16


TWO_PI = 2.0 * math.pi
ENV_COEF = 2.0 * math.pi * math.pi
NU_ZERO = 50000000.0
NU_STEP = 36621.09375
NU_REF = 100000000.0


def wave_numbers(block, start, count):
    index = block * BLOCK_CHANNELS + start + jnp.arange(count, dtype=jnp.int32)
    return (NU_ZERO + index.astype(jnp.float32) * NU_STEP) / NU_REF


def phase_table(xs, ys, lpos, mpos, ks):
    theta = (xs[:, None, None] * lpos[None, None, :] + ys[:, None, None] * mpos[None, None, :]) * (
        -TWO_PI * ks
    )[None, :, None]
    return jnp.stack([jnp.cos(theta), jnp.sin(theta)], axis=1)


def scale_terms(sums, amplitude, widths, residual_norm):
    grad_amp = -residual_norm * sums[0]
    grad_l = -residual_norm * TWO_PI * amplitude * sums[2]
    grad_m = -residual_norm * TWO_PI * amplitude * sums[3]
    grad_w = residual_norm * 2.0 * TWO_PI * math.pi * amplitude * widths * sums[1]
    return jnp.stack([grad_amp, grad_l, grad_m, grad_w])


def model_terms(table, chan, pidx, qidx, r2, kval, amplitude, widths):
    gre = table[:, 0, chan]
    gim = table[:, 1, chan]
    gp_r = jnp.take(gre, pidx, axis=0)
    gp_i = jnp.take(gim, pidx, axis=0)
    gq_r = jnp.take(gre, qidx, axis=0)
    gq_i = jnp.take(gim, qidx, axis=0)
    env = jnp.exp(-(ENV_COEF * kval * kval) * r2[:, None] * (widths * widths)[None, :])
    ep_r = env * (gp_r * gq_r + gp_i * gq_i)
    ep_i = env * (gp_i * gq_r - gp_r * gq_i)
    highest = lax.Precision.HIGHEST
    vr = jnp.dot(ep_r, amplitude, precision=highest, preferred_element_type=jnp.float32)
    vi = jnp.dot(ep_i, amplitude, precision=highest, preferred_element_type=jnp.float32)
    return (ep_r, ep_i, jnp.stack([vr, vi]))


def grad_terms(ep_r, ep_i, rr, ri, wt, kval, dx, dy, r2):
    wr = wt * rr
    wi = wt * ri
    k2r2 = kval * kval * r2
    kdx = kval * dx
    kdy = kval * dy
    left_r = jnp.stack([wr, k2r2 * wr, -kdx * wi, -kdy * wi])
    left_i = jnp.stack([wi, k2r2 * wi, kdx * wr, kdy * wr])
    highest = lax.Precision.HIGHEST
    term = jnp.dot(left_r, ep_r, precision=highest, preferred_element_type=jnp.float32)
    return term + jnp.dot(left_i, ep_i, precision=highest, preferred_element_type=jnp.float32)


def on_device(
    observed, weights, pairs, positions, centres, assign, amplitude, offsets, widths, block_index
):
    ch_dev = observed.shape[1]
    bl_dev = observed.shape[2]
    sources = centres.shape[1]
    onehot = (assign[None, :] == jnp.arange(sources, dtype=jnp.int32)[:, None]).astype(jnp.float32)
    lpos = jnp.sum(onehot * centres[0][:, None], axis=0) + offsets[0]
    mpos = jnp.sum(onehot * centres[1][:, None], axis=0) + offsets[1]
    start = lax.axis_index("ch") * ch_dev
    ks = wave_numbers(block_index[0], start, ch_dev)
    residual_norm = 1.0 / math.sqrt(bl_dev * lax.axis_size("bl") * BLOCK_CHANNELS)
    own = phase_table(positions[:, 0], positions[:, 1], lpos, mpos, ks)
    table, sites_all = (
        lax.all_gather(own, "bl", axis=0, tiled=True),
        lax.all_gather(positions, "bl", axis=0, tiled=True),
    )
    pidx = pairs[0]
    qidx = pairs[1]
    dx = sites_all[pidx, 0] - sites_all[qidx, 0]
    dy = sites_all[pidx, 1] - sites_all[qidx, 1]
    r2 = dx * dx + dy * dy
    totals = jnp.zeros((4, amplitude.shape[0]), jnp.float32)
    fields = []
    parts = []
    for chan in range(ch_dev):
        ep_r, ep_i, part = model_terms(table, chan, pidx, qidx, r2, ks[chan], amplitude, widths)
        fields.append((ep_r, ep_i))
        parts.append(part)
    model = lax.psum(jnp.stack(parts, axis=1), "src")
    visibility_misfit = observed - model
    for chan in range(ch_dev):
        totals = totals + grad_terms(
            fields[chan][0],
            fields[chan][1],
            visibility_misfit[0, chan],
            visibility_misfit[1, chan],
            weights[chan],
            ks[chan],
            dx,
            dy,
            r2,
        )
    summed = lax.psum(totals, ("bl", "ch"))
    grad_comp = scale_terms(summed, amplitude, widths, residual_norm)
    centre_part = jnp.stack(
        [
            jnp.sum(onehot * grad_comp[1][None, :], axis=1),
            jnp.sum(onehot * grad_comp[2][None, :], axis=1),
        ]
    )
    grad_centre = lax.psum(centre_part, "src")
    return (grad_comp, grad_centre, visibility_misfit)


def solution(mesh):
    placed = (
        P(None, "ch", "bl"),
        P("ch", "bl"),
        P(None, "bl"),
        P("bl", None),
        P(),
        P("src"),
        P("src"),
        P(None, "src"),
        P("src"),
        P(),
    )
    return jax.shard_map(
        on_device,
        mesh=mesh,
        in_specs=placed,
        out_specs=(P(None, "src"), P(), P(None, "ch", "bl")),
        check_vma=False,
    )
```

profile of v0, /device:TPU:1, one launch (start us, length us, event | category | flops | bytes accessed | tf_op | source)
XLA Modules:
  0.0 505.5 jit_solution(8787175494387250793)
XLA Ops:
  7.9 0.8 slice_bitcast_fusion.16
  8.6 0.8 fusion.106
  9.4 0.8 slice_bitcast_fusion.19
  10.1 0.8 select_reduce_fusion.3
  11.3 0.7 pad_maximum_fusion
  12.0 0.6 fusion.107
  20.3 0.8 mul.821
  21.1 46.0 %all-gather = f32[32,16,2]{1,2,0:T(2,128)S(1)} all-gather(f32[1,16,2]{1,2,0:T(2,128)} %bitcast.192), channel_id=1, replica_groups=mesh['src'=2,'bl'=32,'ch'=4] {'bl'}, dimensions={0}, use_global_device_ids=true | all-gather | bytes 4224 | tf_op jit(solution)/shard_map/all_gather | solution.py:82
  67.2 0.8 broadcast_or_fusion
  68.0 4.8 gather_fusion
  72.8 4.8 gather_fusion.1
  77.7 4.8 gather_fusion.2
  82.5 4.8 gather_fusion.3
  90.1 2.6 broadcast_multiply_fusion
  92.7 2.6 broadcast_multiply_fusion.1
  95.3 3.6 slice_bitcast_fusion.5
  98.9 3.3 gather_fusion.7
  102.2 3.3 gather_fusion.6
  105.5 3.3 gather_fusion.5
  108.7 3.3 gather_fusion.4
  112.0 2.2 gather_fusion.8
  114.2 2.2 gather_fusion.9
  116.5 2.2 gather_fusion.11
  118.7 2.2 gather_fusion.10
  120.9 2.3 gather_fusion.12
  123.2 2.2 gather_fusion.13
  125.4 2.2 gather_fusion.15
  127.6 2.2 gather_fusion.14
  129.9 1.6 gather_fusion.19
  131.4 1.6 gather_fusion.18
  133.0 1.6 gather_fusion.17
  134.6 1.8 gather_fusion.16
  136.8 0.5 fusion.115
  137.3 0.6 fusion.114
  138.5 2.3 subtract_multiply_fusion.3
  140.9 0.5 fusion.113
  141.4 0.6 fusion.112
  142.0 0.6 fusion.111
  142.5 0.6 fusion.110
  143.1 0.6 fusion.109
  143.7 0.6 fusion.108
  144.3 13.0 %psum.21 = f32[2,4,512]{2,0,1:T(2,128)S(1)} all-reduce(f32[2,4,512]{2,0,1:T(2,128)S(1)} %pad_maximum_fusion.1), channel_id=1, replica_groups=mesh['src'=2,'bl'=32,'ch'=4] {'src'}, use_global_device_ids=true, to_apply=%region_2.0 | all-reduce | flops 4096 | bytes 32768 | tf_op jit(solution)/shard_map/psum | solution.py:96
  157.4 0.6 copy.28
  158.0 1.3 fusion.3
  159.4 1.3 fusion.18
  162.8 326.5 %psum.22 = f32[4,256]{1,0:T(4,128)S(1)} all-reduce(f32[4,256]{1,0:T(4,128)S(1)} %fusion), channel_id=1, replica_groups=mesh['src'=2,'bl'=32,'ch'=4] {'bl','ch'}, use_global_device_ids=true, to_apply=%region_3.5 | all-reduce | flops 1024 | bytes 8192 | tf_op jit(solution)/shard_map/psum | solution.py:110
  489.5 8.5 %psum.23 = f32[2,32]{1,0:T(2,128)} all-reduce(f32[2,32]{1,0:T(2,128)S(1)} %pad_maximum_fusion.3), channel_id=1, replica_groups=mesh['src'=2,'bl'=32,'ch'=4] {'src'}, use_global_device_ids=true, to_apply=%region_6.8 | all-reduce | flops 64 | bytes 512 | tf_op jit(solution)/shard_map/psum | solution.py:118
  498.0 0.6 pad_maximum_fusion.2
  (73 shorter events, 4.0 us)
Async XLA Ops:
  7.2 88.1 %all-gather.3.cloned.1.call-start = ((), (), s32[]{:S(2)}) async-start(), calls=%async_computation | async-start | bytes 4325376 | tf_op jit(solution)/shard_map/all_gather | solution.py:81
  68.0 22.0 %copy-start.12 = (s32[2,512]{1,0:T(2,128)S(1)}, s32[2,512]{1,0:T(2,128)}, u32[]{:S(2)}) copy-start(s32[2,512]{1,0:T(2,128)} %param.14) | copy-start | bytes 12292
  134.6 2.2 copy-start.10
  136.4 1.5 copy-start.2
  136.4 1.5 copy-start.3
  136.4 1.5 copy-start.4
  136.4 1.5 copy-start.5
  136.4 1.6 copy-start.6
  136.4 1.8 copy-start.7
  136.4 1.9 copy-start.8
  136.4 2.1 copy-start.9
  138.5 18.8 %copy-start.11 = (f32[2,4,512]{2,1,0:T(4,128)S(1)}, f32[2,4,512]{2,1,0:T(4,128)}, u32[]{:S(2)}) copy-start(f32[2,4,512]{2,1,0:T(4,128)} %param.12) | copy-start | bytes 49156
  138.5 19.4 %copy-start.14 = (f32[4,512]{1,0:T(4,128)S(1)}, f32[4,512]{1,0:T(4,128)}, u32[]{:S(2)}) copy-start(f32[4,512]{1,0:T(4,128)} %param.13) | copy-start | bytes 24580
  140.8 1.7 copy-start
  140.9 2.8 copy-start.1
  140.9 348.5 %copy-start.13 = (f32[256]{0:T(256)S(1)}, f32[256]{0:T(256)}, u32[]{:S(2)}) copy-start(f32[256]{0:T(256)} %param.20) | copy-start | bytes 3076
  140.9 348.5 %copy-start.15 = (s32[256]{0:T(256)S(1)}, s32[256]{0:T(256)}, u32[]{:S(2)}) copy-start(s32[256]{0:T(256)} %param.17) | copy-start | bytes 3076
Sparse Core Ops, SparseCore 0:
  12.1 67.1 all-gather.2
where the time goes:
time: 515 us; the launch traced here: 505 us
  blocking collectives  394 us (77%)
  local copies, waits for them, and re-layouts  64.6 us (13%)
  between operations  25.4 us (5%)
  other arithmetic  12.3 us (2%)
  matrix products  8.95 us (2%)
    psum x1, blocking collectives, on_device(): summed = lax.psum(totals, ('bl', 'ch'))  327 us
    all_gather x1, blocking collectives, on_device(): lax.all_gather(positions, 'bl', axis=0, tiled=True)  46 us
    psum x1, blocking collectives, on_device(): model = lax.psum(jnp.stack(parts, axis=1), 'src')  13 us
  transfers between devices with their start and end apart: 1, of which 0 were waited for; matrix products, arithmetic and copies ran while one was open for 5% of the time, Pallas kernels for 0%

commit v1 on v0

v1 whole, which is shorter than its diff:
```python
import functools
import math

import jax
import jax.numpy as jnp
from jax import lax
from jax.experimental import pallas as pl
from jax.experimental.pallas import tpu as pltpu
from jax.sharding import PartitionSpec as P

F32 = jnp.float32
BF16 = jnp.bfloat16
LOGICAL = pl.DeviceIdType.LOGICAL
BLOCK_CHANNELS = 16
NU_ZERO = 50000000.0
NU_STEP = 36621.09375
NU_REF = 100000000.0
DK = NU_STEP / NU_REF
CHANS = 4
TWO_PI = 2.0 * math.pi
ENV_COEF = 2.0 * math.pi * math.pi

SIN_COEFS = (4.44288283, -7.30824115, 3.60628896, -0.8457636, 0.10920575)
COS_COEFS = (-1.4142135, 6.97885099, -5.73946117, 1.88356299, -0.31069819)

TERMS = (
    [(a, n - a, 0) for n in range(4) for a in range(n, -1, -1)]
    + [(a, n - a, 1) for n in range(3) for a in range(n, -1, -1)]
    + [(a, n - a, 2) for n in range(2) for a in range(n, -1, -1)]
)
ROWS = 24

Z_STEPS = (-2, 1, -1, 0)
STEPS = (2, 1, -1, 0)


def hops(off):
    return abs(off[0]) + abs(off[1]) + abs(off[2]) + 0.1 * off[3]


def far_first(offs):
    return sorted((o for o in offs if o != (0, 0, 0, 0)), key=lambda o: (hops(o), o), reverse=True)


GATHER = far_first([(dx, 0, dz, dc) for dx in STEPS for dz in Z_STEPS for dc in (0, 1)])
COLUMN = far_first([(0, 0, dz, dc) for dz in (4, 3, 2, 1, 0, -1, -2, -3) for dc in (0, 1)])
PLANE = far_first([(dx, dy, 0, 0) for dx in STEPS for dy in STEPS])
PARTNER = (0, 0, 4, 0)
SENDS_TO_ME = far_first(
    {((-dx + 1) % 4 - 1, (-dy + 1) % 4 - 1, (-dz + 3) % 8 - 3, dc) for dx, dy, dz, dc in GATHER + COLUMN + PLANE}
)


def here():
    bl = lax.axis_index("bl")
    src = lax.axis_index("src")
    return lax.div(bl, 8), lax.axis_index("ch"), src * 4 + lax.rem(lax.div(bl, 2), 4), lax.rem(bl, 2)


def device(me, off):
    x, y, z, core = me
    dx, dy, dz, dc = off
    x = lax.rem(x + (dx + 4), 4) if dx else x
    y = lax.rem(y + (dy + 4), 4) if dy else y
    z = lax.rem(z + (dz + 8), 8) if dz else z
    core = 1 - core if dc else core
    return lax.div(z, 4) * 128 + (x * 8 + lax.rem(z, 4) * 2 + core) * 4 + y


def slot_of(off):
    dx, _, dz, dc = off
    return (dx % 4) * 8 + (dz % 4) * 2 + dc


def rows_iota(shape):
    return lax.broadcasted_iota(jnp.int32, shape, 0)


def one_of(rows, wanted):
    mask = None
    for w in wanted:
        mask = (rows == w) if mask is None else (mask | (rows == w))
    return mask


def pick(rows, pairs, other=0.0):
    out = other
    for wanted, value in pairs:
        if wanted:
            out = jnp.where(one_of(rows, wanted), value, out)
    return out


def monomials(u, v, w, shape):
    rows = rows_iota(shape)

    def power(base, which, top):
        out = jnp.ones(shape, F32)
        p = base
        for n in range(1, top + 1):
            wanted = [j for j, t in enumerate(TERMS) if t[which] == n]
            out = jnp.where(one_of(rows, wanted), jnp.broadcast_to(p, shape), out)
            p = p * base
        return out

    prod = power(u, 0, 3) * power(v, 1, 3) * power(w, 2, 2)
    return jnp.where(rows < len(TERMS), prod, 0.0)


def channel_factors(k_mid, lanes):
    shape = (ROWS, lanes)
    rows = rows_iota(shape)
    consts = []
    for j, (a, b, e) in enumerate(TERMS):
        n = a + b
        sign = -1.0 if (n // 2) % 2 else 1.0
        consts.append(([j], sign * TWO_PI**n / (math.factorial(a) * math.factorial(b) * math.factorial(e))))
    base = pick(rows, consts) + jnp.zeros(shape, F32)
    out = []
    for f in range(CHANS):
        delta = (f - 0.5 * (CHANS - 1)) * DK
        kappa = (-ENV_COEF * delta) * (2.0 * k_mid + delta)
        phase = pick(
            rows,
            [([j for j, t in enumerate(TERMS) if t[0] + t[1] == n], delta**n) for n in range(1, 4)],
            1.0,
        )
        env = jnp.where(
            one_of(rows, [j for j, t in enumerate(TERMS) if t[2] == 1]),
            kappa,
            jnp.where(one_of(rows, [j for j, t in enumerate(TERMS) if t[2] == 2]), kappa * kappa, 1.0),
        )
        out.append(base * phase * env)
    return out


def split2(x):
    high = x.astype(BF16)
    return high, (x - high.astype(F32)).astype(BF16)


def split3(x):
    high = x.astype(BF16)
    rest = x - high.astype(F32)
    mid = rest.astype(BF16)
    return high, mid, (rest - mid.astype(F32)).astype(BF16)


def kernel(
    obs_h, wts_h, pairs_h, pos_h, cen_h, asg_h, amp_h, off_h, wid_h, blk_s,
    comp_o, centre_o, res_o,
    obs_v, wts_v, pairs_v, pos_v, cen_v, asg_v, amp_v, off_v, wid_v,
    table, comp, lcol, mcol, wcol, ep, part, recv_a, part_b, recv_b, resid,
    in_sem, gat_s, gat_r, cmp_s, cmp_r, res_s, res_r, a_s, a_r, b_s, b_r,
):
    me = here()
    x_me, y_me, z_me, core_me = me
    src = lax.axis_index("src")
    z_low = lax.rem(z_me, 4)
    half = src * 256
    barrier = pltpu.get_barrier_semaphore()
    for off in SENDS_TO_ME:
        pl.semaphore_signal(barrier, 1, device_id=device(me, off), device_id_type=LOGICAL)

    halves = pl.ds(pl.multiple_of(half, 256), 256)
    loads = [
        pltpu.make_async_copy(a, b, in_sem.at[i])
        for i, (a, b) in enumerate(
            [
                (pos_h, pos_v), (cen_h, cen_v), (asg_h, asg_v), (amp_h, amp_v), (off_h, off_v), (wid_h, wid_v),
                (pairs_h.at[:, halves], pairs_v), (obs_h.at[:, :, halves], obs_v), (wts_h.at[:, halves], wts_v),
            ]
        )
    ]
    for load in loads:
        load.start()

    loads[0].wait()
    lane = lax.broadcasted_iota(jnp.int32, (16, 128), 1)
    sub = rows_iota((16, 128))
    spread = jnp.where(lane == sub, pos_v[:, 0:1], 0.0) + jnp.where(lane == sub + 16, pos_v[:, 1:2], 0.0)
    table[0] = jnp.sum(spread, axis=0, keepdims=True)

    for load in loads[1:6]:
        load.wait()
    assign = asg_v[...]
    onehot = (jnp.broadcast_to(assign, (32, 256)) == rows_iota((32, 256))).astype(BF16)
    cen_parts = split3(cen_v[...])
    centre = sum(jnp.dot(p, onehot, preferred_element_type=F32) for p in cen_parts)
    lm = centre + off_v[...]
    width = wid_v[...]
    rows8 = rows_iota((8, 256))
    comp[src] = pick(
        rows8,
        [
            ([0], lm[0:1, :]), ([1], lm[1:2, :]), ([2], width * width), ([3], amp_v[...]), ([4], width),
            ([5], assign.astype(F32)),
        ],
    )

    pl.semaphore_wait(barrier, len(SENDS_TO_ME))

    send_comp = pltpu.make_async_remote_copy(
        src_ref=comp.at[src], dst_ref=comp.at[src], send_sem=cmp_s, recv_sem=cmp_r,
        device_id=device(me, PARTNER), device_id_type=LOGICAL,
    )
    send_comp.start()
    for off in GATHER:
        pltpu.make_async_remote_copy(
            src_ref=table.at[0], dst_ref=table.at[slot_of(off)], send_sem=gat_s, recv_sem=gat_r,
            device_id=device(me, off), device_id_type=LOGICAL,
        ).start()

    first = blk_s[0] * BLOCK_CHANNELS + lax.axis_index("ch") * CHANS
    k_mid = (NU_ZERO + (first.astype(F32) + 0.5 * (CHANS - 1)) * NU_STEP) / NU_REF
    ks = [(NU_ZERO + (first + f).astype(F32) * NU_STEP) / NU_REF for f in range(CHANS)]
    gs = channel_factors(k_mid, 256)
    loads[6].wait()
    ant = pairs_v[...]
    shard = lax.shift_right_logical(ant, 4)
    slot = (
        ((x_me - lax.shift_right_logical(shard, 3)) & 3) * 8
        + ((z_low - lax.shift_right_logical(shard, 1)) & 3) * 2
        + ((core_me - shard) & 1)
    )
    inner = ant & 15
    rows32 = rows_iota((32, 128))

    send_comp.wait_recv()
    both = jnp.concatenate([comp[0], comp[1]], axis=1)
    l_row, m_row, w2_row = both[0:1, :], both[1:2, :], both[2:3, :]
    amp_row, w_row = both[3:4, :], both[4:5, :]
    mono = monomials(l_row, m_row, w2_row, (ROWS, 512))
    amp_high, amp_low = split2(mono * amp_row)
    mono_amp = jnp.concatenate([amp_high, amp_low], axis=0)
    cols = jnp.transpose(both)
    lcol[...] = jnp.broadcast_to(cols[:, 0:1], (512, 128))
    mcol[...] = jnp.broadcast_to(cols[:, 1:2], (512, 128))
    wcol[...] = jnp.broadcast_to(cols[:, 2:3], (512, 128))

    pltpu.make_async_copy(table.at[pl.ds(1, 31)], table.at[pl.ds(1, 31)], gat_r).wait()
    sites = table[:, 0, :]
    delta_x, delta_y = [], []
    for t in range(2):
        lanes = slice(128 * t, 128 * t + 128)
        got = []
        for shift in (0, 16):
            total = 0.0
            for a in range(2):
                idx = jnp.broadcast_to(inner[a : a + 1, lanes] + shift, (32, 128))
                val = jnp.take_along_axis(sites, idx, axis=1, mode="promise_in_bounds")
                val = jnp.where(jnp.broadcast_to(slot[a : a + 1, lanes], (32, 128)) == rows32, val, 0.0)
                total = total + val if a == 0 else total - val
            got.append(jnp.sum(total, axis=0, keepdims=True))
        delta_x.append(got[0])
        delta_y.append(got[1])
    dx = jnp.concatenate(delta_x, axis=1)
    dy = jnp.concatenate(delta_y, axis=1)
    r2 = dx * dx + dy * dy

    kx = [k_mid * d for d in delta_x]
    ky = [k_mid * d for d in delta_y]
    er = [
        (-ENV_COEF * math.log2(math.e)) * (k_mid * k_mid) * (delta_x[t] * delta_x[t] + delta_y[t] * delta_y[t])
        for t in range(2)
    ]

    for i in range(32):
        rows = slice(16 * i, 16 * i + 16)
        lc, mc, wc = lcol[rows, :], mcol[rows, :], wcol[rows, :]
        for t in range(2):
            turns = lc * kx[t] + mc * ky[t]
            env = jnp.exp2(wc * er[t])
            r = turns - jnp.round(turns)
            y = r * r
            s = SIN_COEFS[-1]
            for coef in SIN_COEFS[-2::-1]:
                s = s * y + coef
            s = s * r
            c = COS_COEFS[-1]
            for coef in COS_COEFS[-2::-1]:
                c = c * y + coef
            ep_r = env * (1.0 - s * s)
            ep_i = env * (s * c)
            lo = 128 * t
            high, low = split2(ep_r)
            ep[rows, lo : lo + 128] = high
            ep[rows, 256 + lo : 384 + lo] = low
            high, low = split2(ep_i)
            ep[rows, 512 + lo : 640 + lo] = high
            ep[rows, 768 + lo : 896 + lo] = low

    m_all = jnp.dot(mono_amp, ep[...], preferred_element_type=F32)
    m_all = m_all[0:ROWS] + m_all[ROWS:]
    m_r = m_all[:, 0:256] + m_all[:, 256:512]
    m_i = m_all[:, 512:768] + m_all[:, 768:1024]
    rows24 = rows_iota((ROWS, 256))
    odd = one_of(rows24, [j for j, t in enumerate(TERMS) if (t[0] + t[1]) % 2])
    base = monomials(dx, dy, r2, (ROWS, 256))
    n_r = base * jnp.where(odd, m_i, m_r)
    n_i = base * jnp.where(odd, -m_r, m_i)
    loads[7].wait()
    loads[8].wait()
    zero = jnp.zeros((ROWS, 256), F32)
    a0, d0, a1, d1, a2, d2 = zero, zero, zero, zero, zero, zero
    resids = []
    for f in range(CHANS):
        v_r = jnp.sum(gs[f] * n_r, axis=0, keepdims=True)
        v_i = jnp.sum(gs[f] * n_i, axis=0, keepdims=True)
        rr = obs_v[0, f : f + 1, :] - v_r
        ri = obs_v[1, f : f + 1, :] - v_i
        resids.append((rr, ri))
        wr = wts_v[f : f + 1, :] * rr
        wi = wts_v[f : f + 1, :] * ri
        k = ks[f]
        a0 += gs[f] * wr
        d0 += gs[f] * wi
        a1 += gs[f] * (k * wr)
        d1 += gs[f] * (k * wi)
        a2 += gs[f] * (k * k * wr)
        d2 += gs[f] * (k * k * wi)
    resid[src] = pick(
        rows8, [([f], resids[f][0]) for f in range(CHANS)] + [([4 + f], resids[f][1]) for f in range(CHANS)]
    )
    send_resid = pltpu.make_async_remote_copy(
        src_ref=resid.at[src], dst_ref=resid.at[src], send_sem=res_s, recv_sem=res_r,
        device_id=device(me, PARTNER), device_id_type=LOGICAL,
    )
    send_resid.start()

    def sides(a, d):
        return jnp.where(odd, -d, a) * base, jnp.where(odd, a, d) * base

    c0, s0 = sides(a0, d0)
    c1, s1 = sides(a1, d1)
    c2, s2 = sides(a2, d2)
    left_r = jnp.concatenate([c0, c2 * r2, -s1 * dx, -s1 * dy], axis=0)
    left_i = jnp.concatenate([s0, s2 * r2, c1 * dx, c1 * dy], axis=0)
    lr = jnp.concatenate(split2(left_r), axis=0)
    li = jnp.concatenate(split2(left_i), axis=0)
    left = jnp.concatenate([lr, lr, li, li], axis=1)
    y_all = lax.dot_general(left, ep[...], (((1,), (1,)), ((), ())), preferred_element_type=F32)
    y_all = y_all[0 : 4 * ROWS] + y_all[4 * ROWS :]
    sums = [
        jnp.sum(y_all[q * ROWS : (q + 1) * ROWS] * mono, axis=0, keepdims=True) for q in range(4)
    ]
    norm = 1.0 / math.sqrt(16384 * BLOCK_CHANNELS)
    grads = [
        -norm * sums[0],
        (-norm * TWO_PI) * amp_row * sums[2],
        (-norm * TWO_PI) * amp_row * sums[3],
        (norm * 2.0 * TWO_PI * math.pi) * amp_row * w_row * sums[1],
    ]

    onehot_all = (jnp.broadcast_to(both[5:6, :], (32, 512)) == rows_iota((32, 512)).astype(F32)).astype(BF16)
    gl, gm = split3(grads[1]), split3(grads[2])
    wide = lax.dot_general(
        jnp.concatenate(list(gl) + list(gm), axis=0), onehot_all, (((1,), (1,)), ((), ())),
        preferred_element_type=F32,
    )
    cen_l = wide[0:1, :] + wide[1:2, :] + wide[2:3, :]
    cen_m = wide[3:4, :] + wide[4:5, :] + wide[5:6, :]
    cen_rows = jnp.concatenate([cen_l, cen_m, jnp.zeros((1, 64), F32)], axis=1)
    for s in range(2):
        rows = rows_iota((8, 128))
        tile = 0.0
        for h in range(2):
            lo = 256 * s + 128 * h
            for q in range(4):
                tile = jnp.where(rows == 4 * h + q, grads[q][:, lo : lo + 128], tile)
        part[s, 0:8, :] = tile
        part[s, 8:16, :] = jnp.broadcast_to(cen_rows, (8, 128))

    for i, off in enumerate(COLUMN):
        to = lax.div(lax.rem(z_me + (off[2] + 8), 8), 4)
        pltpu.make_async_remote_copy(
            src_ref=part.at[to], dst_ref=recv_a.at[i], send_sem=a_s, recv_sem=a_r,
            device_id=device(me, off), device_id_type=LOGICAL,
        ).start()
    pltpu.make_async_copy(recv_a, recv_a, a_r).wait()
    total = part[src]
    for i in range(15):
        total = total + recv_a[i]
    part_b[...] = total
    for i, off in enumerate(PLANE):
        pltpu.make_async_remote_copy(
            src_ref=part_b, dst_ref=recv_b.at[i], send_sem=b_s, recv_sem=b_r,
            device_id=device(me, off), device_id_type=LOGICAL,
        ).start()
    send_resid.wait_recv()
    for h in range(2):
        res_o[0, :, 256 * h : 256 * h + 256] = resid[h, 0:4, :]
        res_o[1, :, 256 * h : 256 * h + 256] = resid[h, 4:8, :]
    pltpu.make_async_copy(recv_b, recv_b, b_r).wait()
    for i in range(15):
        total = total + recv_b[i]
    comp_o[:, 0:128] = total[0:4, :]
    comp_o[:, 128:256] = total[4:8, :]
    centre_o[0:1, :] = total[8:9, 0:32]
    centre_o[1:2, :] = total[8:9, 32:64]

    send_comp.wait_send()
    send_resid.wait_send()
    pltpu.make_async_copy(table.at[pl.ds(1, 31)], table.at[pl.ds(1, 31)], gat_s).wait()
    pltpu.make_async_copy(recv_a, recv_a, a_s).wait()
    pltpu.make_async_copy(recv_b, recv_b, b_s).wait()


def on_device(observed, weights, pairs, positions, centres, assign, amplitude, offsets, widths, block_index):
    dma = pltpu.SemaphoreType.DMA
    return pl.pallas_call(
        kernel,
        out_shape=(
            jax.ShapeDtypeStruct((4, 256), F32),
            jax.ShapeDtypeStruct((2, 32), F32),
            jax.ShapeDtypeStruct((2, 4, 512), F32),
        ),
        in_specs=[pl.BlockSpec(memory_space=pl.ANY)] * 9 + [pl.BlockSpec(memory_space=pltpu.SMEM)],
        out_specs=tuple([pl.BlockSpec(memory_space=pltpu.VMEM)] * 3),
        scratch_shapes=[
            pltpu.VMEM((2, 4, 256), F32),
            pltpu.VMEM((4, 256), F32),
            pltpu.VMEM((2, 256), jnp.int32),
            pltpu.VMEM((16, 2), F32),
            pltpu.VMEM((2, 32), F32),
            pltpu.VMEM((1, 256), jnp.int32),
            pltpu.VMEM((1, 256), F32),
            pltpu.VMEM((2, 256), F32),
            pltpu.VMEM((1, 256), F32),
            pltpu.VMEM((32, 1, 128), F32),
            pltpu.VMEM((2, 8, 256), F32),
            pltpu.VMEM((512, 128), F32),
            pltpu.VMEM((512, 128), F32),
            pltpu.VMEM((512, 128), F32),
            pltpu.VMEM((512, 1024), BF16),
            pltpu.VMEM((2, 16, 128), F32),
            pltpu.VMEM((15, 16, 128), F32),
            pltpu.VMEM((16, 128), F32),
            pltpu.VMEM((15, 16, 128), F32),
            pltpu.VMEM((2, 8, 256), F32),
            dma((9,)),
        ]
        + [dma(())] * 10,
        compiler_params=pltpu.CompilerParams(
            collective_id=0, has_side_effects=True, vmem_limit_bytes=32 * 1024 * 1024
        ),
        name="refit",
    )(
        observed, weights, pairs, positions, centres, assign.reshape(1, 256), amplitude.reshape(1, 256), offsets,
        widths.reshape(1, 256), block_index,
    )


def solution(mesh):
    placed = (
        P(None, "ch", "bl"),
        P("ch", "bl"),
        P(None, "bl"),
        P("bl", None),
        P(),
        P("src"),
        P("src"),
        P(None, "src"),
        P("src"),
        P(),
    )
    return jax.shard_map(
        on_device,
        mesh=mesh,
        in_specs=placed,
        out_specs=(P(None, "src"), P(), P(None, "ch", "bl")),
        check_vma=False,
    )
```

time: 515 us -> 36.4 us (0.07); the launches traced: 505 us -> 36.1 us
  blocking collectives: 394 us -> 0 us
  local copies, waits for them, and re-layouts: 64.6 us -> 7.3 us
  Pallas kernels: 0 us -> 27.5 us
  between operations: 25.4 us -> 1.31 us
  other arithmetic: 12.3 us -> 0 us
  matrix products: 8.95 us -> 0 us
    psum x3 -> x0, blocking collectives: 348 us -> none  [the longest x1 327 us: on_device(): summed = lax.psum(totals, ('bl', 'ch'))]
    gather x20 -> x0, local copies, waits for them, and re-layouts: 56.8 us -> none  [the longest x2 9.69 us: on_device(): dy = sites_all[pidx, 1] - sites_all[qidx, 1]]
    all_gather x1 -> x0, blocking collectives: 46 us -> none  [on_device(): lax.all_gather(positions, 'bl', axis=0, tiled=True)]
    pallas_call x0 -> x1, Pallas kernels: none -> 27.5 us  [on_device(): pl.pallas_call(kernel, out_shape=(jax.ShapeDtypeStruct((4, 256), F32), ja...]
    dot_general x16 -> x0, matrix products: 8.95 us -> none  [the longest x4 3.22 us: grad_terms(): jnp.dot(left_r, ep_r, precision=highest, preferred_element_type=jnp.float32)]
    mul x16 -> x0, other arithmetic: 8.82 us -> none  [the longest x1 2.58 us: grad_terms(): kdy = kval * dy]
    unnamed x34 -> x20, local copies, waits for them, and re-layouts: 1.36 us -> 7.3 us
  transfers between devices with their start and end apart: 1 -> 0, of which waited for: 0 -> 0; matrix products, arithmetic and copies ran while one was open for 5% -> 0% of each run, Pallas kernels for 0% -> 0%
where the time goes in v1:
time: 36.4 us; the launch traced here: 36.1 us
  Pallas kernels  27.5 us (76%)
  local copies, waits for them, and re-layouts  7.3 us (20%)
  between operations  1.31 us (4%)
    pallas_call x1, Pallas kernels, on_device(): pl.pallas_call(kernel, out_shape=(jax.ShapeDtypeStruct((4, 256), F32), ja...  27.5 us
    unnamed x20, local copies, waits for them, and re-layouts  7.3 us

profile of v1, /device:TPU:1, one launch (start us, length us, event | category | flops | bytes accessed | tf_op | source)
XLA Modules:
  0.0 36.1 jit_solution(8455824454929264287)
XLA Ops:
  0.6 0.0 copy-start
  1.3 0.8 %copy.13.pos_h = f32[16,2]{1,0:T(8,128)S(1)} copy(f32[16,2]{0,1:T(2,128)} %param.13) | data formatting | bytes 256 | tf_op args[3]
  2.1 0.0 copy-done
  2.1 0.0 copy-start.1
  2.1 0.7 %copy-done.1 = f32[4,512]{1,0:T(4,128)S(1)} copy-done((f32[4,512]{1,0:T(4,128)S(1)}, f32[4,512]{1,0:T(4,128)}, u32[]{:S(2)}) %copy-start.1) | copy-done | bytes 8216
  2.8 0.0 copy-start.2
  2.8 0.7 %copy-done.2 = s32[2,512]{1,0:T(2,128)S(1)} copy-done((s32[2,512]{1,0:T(2,128)S(1)}, s32[2,512]{1,0:T(2,128)}, u32[]{:S(2)}) %copy-start.2) | copy-done | bytes 4120
  3.4 0.0 copy-start.3
  3.4 0.7 %copy-done.3 = f32[2,256]{1,0:T(2,128)S(1)} copy-done((f32[2,256]{1,0:T(2,128)S(1)}, f32[2,256]{1,0:T(2,128)}, u32[]{:S(2)}) %copy-start.3) | copy-done | bytes 2072
  4.1 0.0 copy-start.4
  4.1 0.7 %copy-done.4 = f32[2,32]{1,0:T(2,128)S(1)} copy-done((f32[2,32]{1,0:T(2,128)S(1)}, f32[2,32]{1,0:T(2,128)}, u32[]{:S(2)}) %copy-start.4) | copy-done | bytes 280
  4.8 0.0 copy-start.5
  4.8 0.7 %copy-done.5 = s32[256]{0:T(256)S(1)} copy-done((s32[256]{0:T(256)S(1)}, s32[256]{0:T(256)}, u32[]{:S(2)}) %copy-start.5) | copy-done | bytes 1048
  5.5 0.0 copy-start.6
  5.5 0.7 %copy-done.6 = f32[256]{0:T(256)S(1)} copy-done((f32[256]{0:T(256)S(1)}, f32[256]{0:T(256)}, u32[]{:S(2)}) %copy-start.6) | copy-done | bytes 1048
  6.2 0.0 copy-start.7
  6.2 0.7 %copy-done.7 = f32[256]{0:T(256)S(1)} copy-done((f32[256]{0:T(256)S(1)}, f32[256]{0:T(256)}, u32[]{:S(2)}) %copy-start.7) | copy-done | bytes 1048
  6.8 27.5 %refit.1 = (f32[4,256]{1,0:T(4,128)S(1)}, f32[2,32]{1,0:T(2,128)S(1)}, f32[2,4,512]{2,1,0:T(4,128)S(1)}) custom-call(f32[2,4,512]{2,1,0:T(4,128)S(1)} %copy-done, f32[4,512]{1,0:T(4,128)S(1)} %copy-done.1, s32[2,512]{1,0:T(2,128)S(1)} %copy-done.2, f32[16,2]{1,0:T(8,128)S(1)} %copy.13.pos_h, f32[2,32]{1,0:T(2,128)S(1)} %copy-done.4, s32[1,256]{1,0:T(1,128)S(1)} %bitcast.3, ...), custom_call_target="tpu_custom_call" | custom-call | tf_op jit(solution)/shard_map/refit/pallas_call | solution.py:411
  34.3 0.6 %copy.18 = f32[4,256]{1,0:T(4,128)} copy(f32[4,256]{1,0:T(4,128)S(1)} %get-tuple-element.6) | data formatting | bytes 8192
  34.9 0.6 %copy.19 = f32[2,32]{1,0:T(2,128)} copy(f32[2,32]{1,0:T(2,128)S(1)} %get-tuple-element.7) | data formatting | bytes 512
  35.5 0.6 %copy.20 = f32[2,4,512]{2,1,0:T(4,128)} copy(f32[2,4,512]{2,1,0:T(4,128)S(1)} %get-tuple-element.8) | data formatting | bytes 32768
Async XLA Ops:
  0.6 1.4 %copy-start = (f32[2,4,512]{2,1,0:T(4,128)S(1)}, f32[2,4,512]{2,1,0:T(4,128)}, u32[]{:S(2)}) copy-start(f32[2,4,512]{2,1,0:T(4,128)} %obs_h.1) | copy-start | bytes 49156
  2.1 0.7 %copy-start.1 = (f32[4,512]{1,0:T(4,128)S(1)}, f32[4,512]{1,0:T(4,128)}, u32[]{:S(2)}) copy-start(f32[4,512]{1,0:T(4,128)} %wts_h.1) | copy-start | bytes 24580
  2.8 0.7 %copy-start.2 = (s32[2,512]{1,0:T(2,128)S(1)}, s32[2,512]{1,0:T(2,128)}, u32[]{:S(2)}) copy-start(s32[2,512]{1,0:T(2,128)} %pairs_h.1) | copy-start | bytes 12292
  3.4 0.7 %copy-start.3 = (f32[2,256]{1,0:T(2,128)S(1)}, f32[2,256]{1,0:T(2,128)}, u32[]{:S(2)}) copy-start(f32[2,256]{1,0:T(2,128)} %off_h.1) | copy-start | bytes 6148
  4.1 0.7 %copy-start.4 = (f32[2,32]{1,0:T(2,128)S(1)}, f32[2,32]{1,0:T(2,128)}, u32[]{:S(2)}) copy-start(f32[2,32]{1,0:T(2,128)} %cen_h.1) | copy-start | bytes 772
  4.8 0.7 %copy-start.5 = (s32[256]{0:T(256)S(1)}, s32[256]{0:T(256)}, u32[]{:S(2)}) copy-start(s32[256]{0:T(256)} %param.15) | copy-start | bytes 3076
  5.5 0.7 %copy-start.6 = (f32[256]{0:T(256)S(1)}, f32[256]{0:T(256)}, u32[]{:S(2)}) copy-start(f32[256]{0:T(256)} %param.16) | copy-start | bytes 3076
  6.2 0.7 %copy-start.7 = (f32[256]{0:T(256)S(1)}, f32[256]{0:T(256)}, u32[]{:S(2)}) copy-start(f32[256]{0:T(256)} %param.18) | copy-start | bytes 3076

commit v2 on v1

--- a/solution.py
+++ b/solution.py
@@ -176,10 +176,7 @@
         load.start()
 
     loads[0].wait()
-    lane = lax.broadcasted_iota(jnp.int32, (16, 128), 1)
-    sub = rows_iota((16, 128))
-    spread = jnp.where(lane == sub, pos_v[:, 0:1], 0.0) + jnp.where(lane == sub + 16, pos_v[:, 1:2], 0.0)
-    table[0] = jnp.sum(spread, axis=0, keepdims=True)
+    table[0] = jnp.concatenate([pos_v[0:1, :], pos_v[1:2, :], jnp.zeros((1, 96), F32)], axis=1)
 
     for load in loads[1:6]:
         load.wait()
@@ -406,22 +403,38 @@
     pltpu.make_async_copy(recv_b, recv_b, b_s).wait()
 
 
+def deliver(*refs):
+    sem = refs[6]
+    moves = [pltpu.make_async_copy(refs[i], refs[3 + i], sem.at[i]) for i in range(3)]
+    for move in moves:
+        move.start()
+    for move in moves:
+        move.wait()
+
+
 def on_device(observed, weights, pairs, positions, centres, assign, amplitude, offsets, widths, block_index):
     dma = pltpu.SemaphoreType.DMA
-    return pl.pallas_call(
+    operands = [
+        pltpu.with_memory_space_constraint(v, pltpu.HBM)
+        for v in (
+            observed, weights, pairs, positions.T, centres, assign.reshape(1, 256), amplitude.reshape(1, 256), offsets,
+            widths.reshape(1, 256),
+        )
+    ]
+    sums = pl.pallas_call(
         kernel,
         out_shape=(
             jax.ShapeDtypeStruct((4, 256), F32),
             jax.ShapeDtypeStruct((2, 32), F32),
             jax.ShapeDtypeStruct((2, 4, 512), F32),
         ),
-        in_specs=[pl.BlockSpec(memory_space=pl.ANY)] * 9 + [pl.BlockSpec(memory_space=pltpu.SMEM)],
+        in_specs=[pl.BlockSpec(memory_space=pltpu.HBM)] * 9 + [pl.BlockSpec(memory_space=pltpu.SMEM)],
         out_specs=tuple([pl.BlockSpec(memory_space=pltpu.VMEM)] * 3),
         scratch_shapes=[
             pltpu.VMEM((2, 4, 256), F32),
             pltpu.VMEM((4, 256), F32),
             pltpu.VMEM((2, 256), jnp.int32),
-            pltpu.VMEM((16, 2), F32),
+            pltpu.VMEM((2, 16), F32),
             pltpu.VMEM((2, 32), F32),
             pltpu.VMEM((1, 256), jnp.int32),
             pltpu.VMEM((1, 256), F32),
@@ -445,10 +458,15 @@
             collective_id=0, has_side_effects=True, vmem_limit_bytes=32 * 1024 * 1024
         ),
         name="refit",
-    )(
-        observed, weights, pairs, positions, centres, assign.reshape(1, 256), amplitude.reshape(1, 256), offsets,
-        widths.reshape(1, 256), block_index,
-    )
+    )(*operands, block_index)
+    return pl.pallas_call(
+        deliver,
+        out_shape=tuple(jax.ShapeDtypeStruct(v.shape, F32) for v in sums),
+        in_specs=[pl.BlockSpec(memory_space=pltpu.VMEM)] * 3,
+        out_specs=tuple([pl.BlockSpec(memory_space=pltpu.HBM)] * 3),
+        scratch_shapes=[dma((3,))],
+        name="deliver",
+    )(*(pltpu.with_memory_space_constraint(v, pltpu.VMEM) for v in sums))
 
 
 def solution(mesh):

time: 36.4 us -> 29.7 us (0.82)
  local copies, waits for them, and re-layouts: 7.3 us -> 0 us
  Pallas kernels: 27.5 us -> 28.3 us
    unnamed x20 -> x0, local copies, waits for them, and re-layouts: 7.3 us -> none
    pallas_call x0 -> x1, Pallas kernels: none -> 0.64 us  [on_device(): pl.pallas_call(deliver, out_shape=tuple((jax.ShapeDtypeStruct(v.shape, F3...]
where the time goes in v2:
time: 29.7 us; the launch traced here: 29.6 us
  Pallas kernels  28.3 us (95%)
  between operations  1.29 us (4%)
    pallas_call x1, Pallas kernels, on_device(): pl.pallas_call(kernel, out_shape=(jax.ShapeDtypeStruct((4, 256), F32), ja...  27.7 us
    pallas_call x1, Pallas kernels, on_device(): pl.pallas_call(deliver, out_shape=tuple((jax.ShapeDtypeStruct(v.shape, F3...  0.64 us

profile of v2, /device:TPU:1, one launch (start us, length us, event | category | flops | bytes accessed | tf_op | source)
XLA Modules:
  0.0 29.6 jit_solution(466965870650065681)
XLA Ops:
  1.3 27.7 %refit.1 = (f32[4,256]{1,0:T(4,128)S(1)}, f32[2,32]{1,0:T(2,128)S(1)}, f32[2,4,512]{2,1,0:T(4,128)S(1)}) custom-call(f32[2,4,512]{2,1,0:T(4,128)} %obs_h.1, f32[4,512]{1,0:T(4,128)} %wts_h.1, s32[2,512]{1,0:T(2,128)} %pairs_h.1, f32[2,16]{1,0:T(2,128)} %bitcast.4, f32[2,32]{1,0:T(2,128)} %cen_h.1, s32[1,256]{1,0:T(1,128)} %bitcast.5, f32[1,256]{1,0:T(1,128)} %bitcast.6, ...), custom_call_target="tpu_custom_call" | custom-call | tf_op jit(solution)/shard_map/refit/pallas_call | solution.py:424
  29.0 0.6 %deliver.1 = (f32[4,256]{1,0:T(4,128)}, f32[2,32]{1,0:T(2,128)}, f32[2,4,512]{2,1,0:T(4,128)}) custom-call(f32[4,256]{1,0:T(4,128)S(1)} %get-tuple-element.6.refs_0_, f32[2,32]{1,0:T(2,128)S(1)} %get-tuple-element.7.refs_1_, f32[2,4,512]{2,1,0:T(4,128)S(1)} %get-tuple-element.8.refs_2_), custom_call_target="tpu_custom_call" | custom-call | tf_op jit(solution)/shard_map/deliver/pallas_call | solution.py:462

commit v3 on v2

--- a/solution.py
+++ b/solution.py
@@ -30,24 +30,20 @@
 )
 ROWS = 24
 
+STEPS = (2, 1, -1, 0)
 Z_STEPS = (-2, 1, -1, 0)
-STEPS = (2, 1, -1, 0)
-
-
-def hops(off):
-    return abs(off[0]) + abs(off[1]) + abs(off[2]) + 0.1 * off[3]
 
 
 def far_first(offs):
-    return sorted((o for o in offs if o != (0, 0, 0, 0)), key=lambda o: (hops(o), o), reverse=True)
-
-
-GATHER = far_first([(dx, 0, dz, dc) for dx in STEPS for dz in Z_STEPS for dc in (0, 1)])
-COLUMN = far_first([(0, 0, dz, dc) for dz in (4, 3, 2, 1, 0, -1, -2, -3) for dc in (0, 1)])
-PLANE = far_first([(dx, dy, 0, 0) for dx in STEPS for dy in STEPS])
-PARTNER = (0, 0, 4, 0)
-SENDS_TO_ME = far_first(
-    {((-dx + 1) % 4 - 1, (-dy + 1) % 4 - 1, (-dz + 3) % 8 - 3, dc) for dx, dy, dz, dc in GATHER + COLUMN + PLANE}
+    return sorted((o for o in offs if o != (0, 0, 0)), key=lambda o: (sum(map(abs, o)), o), reverse=True)
+
+
+GATHER = far_first([(dx, 0, dz) for dx in STEPS for dz in Z_STEPS])
+COLUMN = far_first([(0, 0, dz) for dz in (4, 3, 2, 1, 0, -1, -2, -3)])
+PLANE = far_first([(dx, dy, 0) for dx in STEPS for dy in STEPS])
+PARTNER = (0, 0, 4)
+GREET = far_first(
+    {((-dx + 1) % 4 - 1, (-dy + 1) % 4 - 1, (-dz + 3) % 8 - 3) for dx, dy, dz in GATHER + COLUMN + PLANE}
 )
 
 
@@ -57,19 +53,27 @@
     return lax.div(bl, 8), lax.axis_index("ch"), src * 4 + lax.rem(lax.div(bl, 2), 4), lax.rem(bl, 2)
 
 
-def device(me, off):
-    x, y, z, core = me
-    dx, dy, dz, dc = off
+def device(me, off, core):
+    x, y, z, _ = me
+    dx, dy, dz = off
     x = lax.rem(x + (dx + 4), 4) if dx else x
     y = lax.rem(y + (dy + 4), 4) if dy else y
     z = lax.rem(z + (dz + 8), 8) if dz else z
-    core = 1 - core if dc else core
     return lax.div(z, 4) * 128 + (x * 8 + lax.rem(z, 4) * 2 + core) * 4 + y
 
 
 def slot_of(off):
-    dx, _, dz, dc = off
-    return (dx % 4) * 8 + (dz % 4) * 2 + dc
+    return (off[0] % 4) * 4 + off[2] % 4
+
+
+def send(src_ref, dst_ref, send_sem, recv_sem, to):
+    return pltpu.make_async_remote_copy(
+        src_ref=src_ref, dst_ref=dst_ref, send_sem=send_sem, recv_sem=recv_sem, device_id=to, device_id_type=LOGICAL
+    )
+
+
+def drain(ref, sem):
+    pltpu.make_async_copy(ref, ref, sem).wait()
 
 
 def rows_iota(shape):
@@ -147,20 +151,23 @@
 
 
 def kernel(
-    obs_h, wts_h, pairs_h, pos_h, cen_h, asg_h, amp_h, off_h, wid_h, blk_s,
+    obs_h, wts_h, pairs_h, pos_h, cen_h, asg_h, amp_h, off_h, wid_h, blk_h,
     comp_o, centre_o, res_o,
-    obs_v, wts_v, pairs_v, pos_v, cen_v, asg_v, amp_v, off_v, wid_v,
-    table, comp, lcol, mcol, wcol, ep, part, recv_a, part_b, recv_b, resid,
-    in_sem, gat_s, gat_r, cmp_s, cmp_r, res_s, res_r, a_s, a_r, b_s, b_r,
+    obs_v, wts_v, pairs_v, pos_v, cen_v, asg_v, amp_v, off_v, wid_v, blk_s,
+    sibling, table, comp, lcol, mcol, wcol, ep, part, recv_a, recv_b, resid,
+    in_sem, sib_s, sib_r, gat_s, gat_r, cmp_s, cmp_r, res_s, res_r, a_s, a_r, b_s, b_r,
 ):
     me = here()
     x_me, y_me, z_me, core_me = me
     src = lax.axis_index("src")
     z_low = lax.rem(z_me, 4)
     half = src * 256
+    here0, here1 = device(me, (0, 0, 0), 0), device(me, (0, 0, 0), 1)
+    is0, is1 = core_me == 0, core_me == 1
     barrier = pltpu.get_barrier_semaphore()
-    for off in SENDS_TO_ME:
-        pl.semaphore_signal(barrier, 1, device_id=device(me, off), device_id_type=LOGICAL)
+    pl.semaphore_signal(barrier, 1, device_id=jnp.where(is0, here1, here0), device_id_type=LOGICAL)
+    for off in GREET:
+        pl.semaphore_signal(barrier, 1, device_id=device(me, off, 1), device_id_type=LOGICAL)
 
     halves = pl.ds(pl.multiple_of(half, 256), 256)
     loads = [
@@ -168,7 +175,7 @@
         for i, (a, b) in enumerate(
             [
                 (pos_h, pos_v), (cen_h, cen_v), (asg_h, asg_v), (amp_h, amp_v), (off_h, off_v), (wid_h, wid_v),
-                (pairs_h.at[:, halves], pairs_v), (obs_h.at[:, :, halves], obs_v), (wts_h.at[:, halves], wts_v),
+                (pairs_h.at[:, halves], pairs_v), (obs_h.at[:, :, halves], obs_v), (wts_h.at[:, halves], wts_v), (blk_h, blk_s),
             ]
         )
     ]
@@ -176,7 +183,19 @@
         load.start()
 
     loads[0].wait()
-    table[0] = jnp.concatenate([pos_v[0:1, :], pos_v[1:2, :], jnp.zeros((1, 96), F32)], axis=1)
+    gap = jnp.zeros((1, 16), F32)
+    xs, ys = pos_v[0:1, :], pos_v[1:2, :]
+    tail = jnp.zeros((1, 64), F32)
+
+    @pl.when(is0)
+    def _():
+        sibling[...] = jnp.concatenate([xs, gap, ys, gap, tail], axis=1)
+        pl.semaphore_wait(barrier, 1)
+        send(sibling, table.at[0], sib_s, sib_r, here1).start()
+
+    @pl.when(is1)
+    def _():
+        sibling[...] = jnp.concatenate([gap, xs, gap, ys, tail], axis=1)
 
     for load in loads[1:6]:
         load.wait()
@@ -195,35 +214,31 @@
         ],
     )
 
-    pl.semaphore_wait(barrier, len(SENDS_TO_ME))
-
-    send_comp = pltpu.make_async_remote_copy(
-        src_ref=comp.at[src], dst_ref=comp.at[src], send_sem=cmp_s, recv_sem=cmp_r,
-        device_id=device(me, PARTNER), device_id_type=LOGICAL,
-    )
-    send_comp.start()
-    for off in GATHER:
-        pltpu.make_async_remote_copy(
-            src_ref=table.at[0], dst_ref=table.at[slot_of(off)], send_sem=gat_s, recv_sem=gat_r,
-            device_id=device(me, off), device_id_type=LOGICAL,
-        ).start()
-
+    @pl.when(is1)
+    def _():
+        drain(table.at[0], sib_r)
+        table[0] = table[0] + sibling[...]
+        pl.semaphore_wait(barrier, 2 * len(GREET) + 1)
+        for core in (0, 1):
+            send(comp.at[src], comp.at[src], cmp_s.at[core], cmp_r, device(me, PARTNER, core)).start()
+        for off in GATHER:
+            for core in (0, 1):
+                send(table.at[0], table.at[slot_of(off)], gat_s.at[core], gat_r, device(me, off, core)).start()
+        send(table.at[0], table.at[0], gat_s.at[0], gat_r, here0).start()
+
+    loads[6].wait()
+    loads[9].wait()
     first = blk_s[0] * BLOCK_CHANNELS + lax.axis_index("ch") * CHANS
     k_mid = (NU_ZERO + (first.astype(F32) + 0.5 * (CHANS - 1)) * NU_STEP) / NU_REF
     ks = [(NU_ZERO + (first + f).astype(F32) * NU_STEP) / NU_REF for f in range(CHANS)]
     gs = channel_factors(k_mid, 256)
-    loads[6].wait()
     ant = pairs_v[...]
-    shard = lax.shift_right_logical(ant, 4)
-    slot = (
-        ((x_me - lax.shift_right_logical(shard, 3)) & 3) * 8
-        + ((z_low - lax.shift_right_logical(shard, 1)) & 3) * 2
-        + ((core_me - shard) & 1)
-    )
-    inner = ant & 15
-    rows32 = rows_iota((32, 128))
-
-    send_comp.wait_recv()
+    chip = lax.shift_right_logical(ant, 5)
+    slot = ((x_me - lax.shift_right_logical(chip, 2)) & 3) * 4 + ((z_low - chip) & 3)
+    inner = ant & 31
+    rows16 = rows_iota((16, 128))
+
+    drain(comp.at[0], cmp_r)
     both = jnp.concatenate([comp[0], comp[1]], axis=1)
     l_row, m_row, w2_row = both[0:1, :], both[1:2, :], both[2:3, :]
     amp_row, w_row = both[3:4, :], both[4:5, :]
@@ -235,18 +250,25 @@
     mcol[...] = jnp.broadcast_to(cols[:, 1:2], (512, 128))
     wcol[...] = jnp.broadcast_to(cols[:, 2:3], (512, 128))
 
-    pltpu.make_async_copy(table.at[pl.ds(1, 31)], table.at[pl.ds(1, 31)], gat_r).wait()
+    @pl.when(is0)
+    def _():
+        drain(table, gat_r)
+
+    @pl.when(is1)
+    def _():
+        drain(table.at[pl.ds(1, 15)], gat_r)
+
     sites = table[:, 0, :]
     delta_x, delta_y = [], []
     for t in range(2):
         lanes = slice(128 * t, 128 * t + 128)
         got = []
-        for shift in (0, 16):
+        for shift in (0, 32):
             total = 0.0
             for a in range(2):
-                idx = jnp.broadcast_to(inner[a : a + 1, lanes] + shift, (32, 128))
+                idx = jnp.broadcast_to(inner[a : a + 1, lanes] + shift, (16, 128))
                 val = jnp.take_along_axis(sites, idx, axis=1, mode="promise_in_bounds")
-                val = jnp.where(jnp.broadcast_to(slot[a : a + 1, lanes], (32, 128)) == rows32, val, 0.0)
+                val = jnp.where(jnp.broadcast_to(slot[a : a + 1, lanes], (16, 128)) == rows16, val, 0.0)
                 total = total + val if a == 0 else total - val
             got.append(jnp.sum(total, axis=0, keepdims=True))
         delta_x.append(got[0])
@@ -319,9 +341,8 @@
     resid[src] = pick(
         rows8, [([f], resids[f][0]) for f in range(CHANS)] + [([4 + f], resids[f][1]) for f in range(CHANS)]
     )
-    send_resid = pltpu.make_async_remote_copy(
-        src_ref=resid.at[src], dst_ref=resid.at[src], send_sem=res_s, recv_sem=res_r,
-        device_id=device(me, PARTNER), device_id_type=LOGICAL,
+    send_resid = send(
+        resid.at[src], resid.at[src], res_s, res_r, jnp.where(is0, device(me, PARTNER, 0), device(me, PARTNER, 1))
     )
     send_resid.start()
 
@@ -368,39 +389,66 @@
         part[s, 0:8, :] = tile
         part[s, 8:16, :] = jnp.broadcast_to(cen_rows, (8, 128))
 
-    for i, off in enumerate(COLUMN):
-        to = lax.div(lax.rem(z_me + (off[2] + 8), 8), 4)
-        pltpu.make_async_remote_copy(
-            src_ref=part.at[to], dst_ref=recv_a.at[i], send_sem=a_s, recv_sem=a_r,
-            device_id=device(me, off), device_id_type=LOGICAL,
-        ).start()
-    pltpu.make_async_copy(recv_a, recv_a, a_r).wait()
-    total = part[src]
-    for i in range(15):
-        total = total + recv_a[i]
-    part_b[...] = total
-    for i, off in enumerate(PLANE):
-        pltpu.make_async_remote_copy(
-            src_ref=part_b, dst_ref=recv_b.at[i], send_sem=b_s, recv_sem=b_r,
-            device_id=device(me, off), device_id_type=LOGICAL,
-        ).start()
+    def column(core):
+        for i, off in enumerate(COLUMN):
+            to = lax.div(lax.rem(z_me + (off[2] + 8), 8), 4)
+            send(part.at[to], recv_a.at[2 * i + core], a_s, a_r, device(me, off, 1)).start()
+
+    @pl.when(is0)
+    def _():
+        column(0)
+        send(part.at[src], recv_a.at[14], a_s, a_r, here1).start()
+
+    @pl.when(is1)
+    def _():
+        column(1)
+        drain(recv_a, a_r)
+        total = part[src]
+        for i in range(15):
+            total = total + recv_a[i]
+        recv_b[0] = total
+        for i, off in enumerate(PLANE):
+            for core in (0, 1):
+                send(recv_b.at[0], recv_b.at[i + 1], b_s.at[core], b_r, device(me, off, core)).start()
+        send(recv_b.at[0], recv_b.at[0], b_s.at[0], b_r, here0).start()
+
     send_resid.wait_recv()
     for h in range(2):
         res_o[0, :, 256 * h : 256 * h + 256] = resid[h, 0:4, :]
         res_o[1, :, 256 * h : 256 * h + 256] = resid[h, 4:8, :]
-    pltpu.make_async_copy(recv_b, recv_b, b_r).wait()
-    for i in range(15):
+
+    @pl.when(is0)
+    def _():
+        drain(recv_b, b_r)
+
+    @pl.when(is1)
+    def _():
+        drain(recv_b.at[pl.ds(1, 15)], b_r)
+
+    total = recv_b[0]
+    for i in range(1, 16):
         total = total + recv_b[i]
     comp_o[:, 0:128] = total[0:4, :]
     comp_o[:, 128:256] = total[4:8, :]
     centre_o[0:1, :] = total[8:9, 0:32]
     centre_o[1:2, :] = total[8:9, 32:64]
 
-    send_comp.wait_send()
     send_resid.wait_send()
-    pltpu.make_async_copy(table.at[pl.ds(1, 31)], table.at[pl.ds(1, 31)], gat_s).wait()
-    pltpu.make_async_copy(recv_a, recv_a, a_s).wait()
-    pltpu.make_async_copy(recv_b, recv_b, b_s).wait()
+
+    @pl.when(is0)
+    def _():
+        drain(sibling, sib_s)
+        drain(recv_a.at[pl.ds(0, 8)], a_s)
+
+    @pl.when(is1)
+    def _():
+        for core in (0, 1):
+            drain(comp.at[0], cmp_s.at[core])
+        drain(table, gat_s.at[0])
+        drain(table.at[pl.ds(1, 15)], gat_s.at[1])
+        drain(recv_a.at[pl.ds(0, 7)], a_s)
+        drain(recv_b, b_s.at[0])
+        drain(recv_b.at[pl.ds(1, 15)], b_s.at[1])
 
 
 def deliver(*refs):
@@ -428,7 +476,7 @@
             jax.ShapeDtypeStruct((2, 32), F32),
             jax.ShapeDtypeStruct((2, 4, 512), F32),
         ),
-        in_specs=[pl.BlockSpec(memory_space=pltpu.HBM)] * 9 + [pl.BlockSpec(memory_space=pltpu.SMEM)],
+        in_specs=[pl.BlockSpec(memory_space=pltpu.HBM)] * 9 + [pl.BlockSpec(memory_space=pl.ANY)],
         out_specs=tuple([pl.BlockSpec(memory_space=pltpu.VMEM)] * 3),
         scratch_shapes=[
             pltpu.VMEM((2, 4, 256), F32),
@@ -440,7 +488,9 @@
             pltpu.VMEM((1, 256), F32),
             pltpu.VMEM((2, 256), F32),
             pltpu.VMEM((1, 256), F32),
-            pltpu.VMEM((32, 1, 128), F32),
+            pltpu.SMEM((1,), jnp.int32),
+            pltpu.VMEM((1, 128), F32),
+            pltpu.VMEM((16, 1, 128), F32),
             pltpu.VMEM((2, 8, 256), F32),
             pltpu.VMEM((512, 128), F32),
             pltpu.VMEM((512, 128), F32),
@@ -448,12 +498,11 @@
             pltpu.VMEM((512, 1024), BF16),
             pltpu.VMEM((2, 16, 128), F32),
             pltpu.VMEM((15, 16, 128), F32),
-            pltpu.VMEM((16, 128), F32),
-            pltpu.VMEM((15, 16, 128), F32),
+            pltpu.VMEM((16, 16, 128), F32),
             pltpu.VMEM((2, 8, 256), F32),
-            dma((9,)),
-        ]
-        + [dma(())] * 10,
+            dma((10,)), dma(()), dma(()), dma((2,)), dma(()), dma((2,)), dma(()), dma(()), dma(()), dma(()), dma(()),
+            dma((2,)), dma(()),
+        ],
         compiler_params=pltpu.CompilerParams(
             collective_id=0, has_side_effects=True, vmem_limit_bytes=32 * 1024 * 1024
         ),

time: 29.7 us -> 28.6 us (0.963)
  Pallas kernels: 28.3 us -> 27.2 us
    pallas_call x1, Pallas kernels: 27.7 us -> 26.5 us  [on_device(): pl.pallas_call(kernel, out_shape=(jax.ShapeDtypeStruct((4, 256), F32), ja...]
where the time goes in v3:
time: 28.6 us; the launch traced here: 28.5 us
  Pallas kernels  27.2 us (95%)
  between operations  1.29 us (5%)
    pallas_call x1, Pallas kernels, on_device(): pl.pallas_call(kernel, out_shape=(jax.ShapeDtypeStruct((4, 256), F32), ja...  26.5 us
    pallas_call x1, Pallas kernels, on_device(): pl.pallas_call(deliver, out_shape=tuple((jax.ShapeDtypeStruct(v.shape, F3...  0.64 us

profile of v3, /device:TPU:1, one launch (start us, length us, event | category | flops | bytes accessed | tf_op | source)
XLA Modules:
  0.0 28.5 jit_solution(4591667258618455269)
XLA Ops:
  1.3 26.5 %refit.1 = (f32[4,256]{1,0:T(4,128)S(1)}, f32[2,32]{1,0:T(2,128)S(1)}, f32[2,4,512]{2,1,0:T(4,128)S(1)}) custom-call(f32[2,4,512]{2,1,0:T(4,128)} %obs_h.1, f32[4,512]{1,0:T(4,128)} %wts_h.1, s32[2,512]{1,0:T(2,128)} %pairs_h.1, f32[2,16]{1,0:T(2,128)} %bitcast.4, f32[2,32]{1,0:T(2,128)} %cen_h.1, s32[1,256]{1,0:T(1,128)} %bitcast.5, f32[1,256]{1,0:T(1,128)} %bitcast.6, ...), custom_call_target="tpu_custom_call" | custom-call | tf_op jit(solution)/shard_map/refit/pallas_call | solution.py:472
  27.8 0.6 %deliver.1 = (f32[4,256]{1,0:T(4,128)}, f32[2,32]{1,0:T(2,128)}, f32[2,4,512]{2,1,0:T(4,128)}) custom-call(f32[4,256]{1,0:T(4,128)S(1)} %get-tuple-element.6.refs_0_, f32[2,32]{1,0:T(2,128)S(1)} %get-tuple-element.7.refs_1_, f32[2,4,512]{2,1,0:T(4,128)S(1)} %get-tuple-element.8.refs_2_), custom_call_target="tpu_custom_call" | custom-call | tf_op jit(solution)/shard_map/deliver/pallas_call | solution.py:511

commit v4 on v3

--- a/solution.py
+++ b/solution.py
@@ -387,7 +387,7 @@
             for q in range(4):
                 tile = jnp.where(rows == 4 * h + q, grads[q][:, lo : lo + 128], tile)
         part[s, 0:8, :] = tile
-        part[s, 8:16, :] = jnp.broadcast_to(cen_rows, (8, 128))
+        part[s, 8:9, :] = cen_rows
 
     def column(core):
         for i, off in enumerate(COLUMN):
@@ -496,9 +496,9 @@
             pltpu.VMEM((512, 128), F32),
             pltpu.VMEM((512, 128), F32),
             pltpu.VMEM((512, 1024), BF16),
-            pltpu.VMEM((2, 16, 128), F32),
-            pltpu.VMEM((15, 16, 128), F32),
-            pltpu.VMEM((16, 16, 128), F32),
+            pltpu.VMEM((2, 9, 128), F32),
+            pltpu.VMEM((15, 9, 128), F32),
+            pltpu.VMEM((16, 9, 128), F32),
             pltpu.VMEM((2, 8, 256), F32),
             dma((10,)), dma(()), dma(()), dma((2,)), dma(()), dma((2,)), dma(()), dma(()), dma(()), dma(()), dma(()),
             dma((2,)), dma(()),

time: 28.6 us -> 28.2 us (0.986)
  Pallas kernels: 27.2 us -> 26.7 us
    pallas_call x1, Pallas kernels: 26.5 us -> 26.1 us  [on_device(): pl.pallas_call(kernel, out_shape=(jax.ShapeDtypeStruct((4, 256), F32), ja...]
where the time goes in v4:
time: 28.2 us; the launch traced here: 28 us
  Pallas kernels  26.7 us (95%)
  between operations  1.29 us (5%)
    pallas_call x1, Pallas kernels, on_device(): pl.pallas_call(kernel, out_shape=(jax.ShapeDtypeStruct((4, 256), F32), ja...  26.1 us
    pallas_call x1, Pallas kernels, on_device(): pl.pallas_call(deliver, out_shape=tuple((jax.ShapeDtypeStruct(v.shape, F3...  0.64 us

profile of v4, /device:TPU:1, one launch (start us, length us, event | category | flops | bytes accessed | tf_op | source)
XLA Modules:
  0.0 28.0 jit_solution(6272806191350967799)
XLA Ops:
  1.3 26.1 %refit.1 = (f32[4,256]{1,0:T(4,128)S(1)}, f32[2,32]{1,0:T(2,128)S(1)}, f32[2,4,512]{2,1,0:T(4,128)S(1)}) custom-call(f32[2,4,512]{2,1,0:T(4,128)} %obs_h.1, f32[4,512]{1,0:T(4,128)} %wts_h.1, s32[2,512]{1,0:T(2,128)} %pairs_h.1, f32[2,16]{1,0:T(2,128)} %bitcast.4, f32[2,32]{1,0:T(2,128)} %cen_h.1, s32[1,256]{1,0:T(1,128)} %bitcast.5, f32[1,256]{1,0:T(1,128)} %bitcast.6, ...), custom_call_target="tpu_custom_call" | custom-call | tf_op jit(solution)/shard_map/refit/pallas_call | solution.py:472
  27.4 0.6 %deliver.1 = (f32[4,256]{1,0:T(4,128)}, f32[2,32]{1,0:T(2,128)}, f32[2,4,512]{2,1,0:T(4,128)}) custom-call(f32[4,256]{1,0:T(4,128)S(1)} %get-tuple-element.6.refs_0_, f32[2,32]{1,0:T(2,128)S(1)} %get-tuple-element.7.refs_1_, f32[2,4,512]{2,1,0:T(4,128)S(1)} %get-tuple-element.8.refs_2_), custom_call_target="tpu_custom_call" | custom-call | tf_op jit(solution)/shard_map/deliver/pallas_call | solution.py:511

commit v5 on v4

--- a/solution.py
+++ b/solution.py
@@ -23,12 +23,16 @@
 SIN_COEFS = (4.44288283, -7.30824115, 3.60628896, -0.8457636, 0.10920575)
 COS_COEFS = (-1.4142135, 6.97885099, -5.73946117, 1.88356299, -0.31069819)
 
+ROUNDER = 12582912.0
+NT = (((1,), (1,)), ((), ()))
+
 TERMS = (
     [(a, n - a, 0) for n in range(4) for a in range(n, -1, -1)]
     + [(a, n - a, 1) for n in range(3) for a in range(n, -1, -1)]
     + [(a, n - a, 2) for n in range(2) for a in range(n, -1, -1)]
 )
 ROWS = 24
+ODD = [j for j, t in enumerate(TERMS) if (t[0] + t[1]) % 2]
 
 STEPS = (2, 1, -1, 0)
 Z_STEPS = (-2, 1, -1, 0)
@@ -95,20 +99,21 @@
     return out
 
 
-def monomials(u, v, w, shape):
+def selectors(shape):
     rows = rows_iota(shape)
-
-    def power(base, which, top):
-        out = jnp.ones(shape, F32)
-        p = base
-        for n in range(1, top + 1):
+    out = []
+    for which, top in ((0, 3), (1, 3), (2, 2)):
+        for n in range(top + 1):
             wanted = [j for j, t in enumerate(TERMS) if t[which] == n]
-            out = jnp.where(one_of(rows, wanted), jnp.broadcast_to(p, shape), out)
-            p = p * base
-        return out
-
-    prod = power(u, 0, 3) * power(v, 1, 3) * power(w, 2, 2)
-    return jnp.where(rows < len(TERMS), prod, 0.0)
+            out.append(jnp.where(one_of(rows, wanted), 1.0, 0.0) + jnp.zeros(shape, F32))
+    return out
+
+
+def monomials(u, v, w, sel):
+    u2, v2 = u * u, v * v
+    p = sel[0] + sel[1] * u + sel[2] * u2 + sel[3] * (u2 * u)
+    q = sel[4] + sel[5] * v + sel[6] * v2 + sel[7] * (v2 * v)
+    return p * q * (sel[8] + sel[9] * w + sel[10] * (w * w))
 
 
 def channel_factors(k_mid, lanes):
@@ -139,8 +144,9 @@
 
 
 def split2(x):
-    high = x.astype(BF16)
-    return high, (x - high.astype(F32)).astype(BF16)
+    wide = x * 65537.0
+    high = wide - (wide - x)
+    return high.astype(BF16), (x - high).astype(BF16)
 
 
 def split3(x):
@@ -154,13 +160,14 @@
     obs_h, wts_h, pairs_h, pos_h, cen_h, asg_h, amp_h, off_h, wid_h, blk_h,
     comp_o, centre_o, res_o,
     obs_v, wts_v, pairs_v, pos_v, cen_v, asg_v, amp_v, off_v, wid_v, blk_s,
-    sibling, table, comp, lcol, mcol, wcol, ep, part, recv_a, recv_b, resid,
+    sibling, table, comp, lcol, mcol, wcol, ep_a, ep_b, ep_c, ep_d, part, recv_a, recv_b, resid, gs_v, sel_v, hot_v,
     in_sem, sib_s, sib_r, gat_s, gat_r, cmp_s, cmp_r, res_s, res_r, a_s, a_r, b_s, b_r,
 ):
     me = here()
     x_me, y_me, z_me, core_me = me
     src = lax.axis_index("src")
     z_low = lax.rem(z_me, 4)
+    at_end = (z_low == 0) | (z_low == 3)
     half = src * 256
     here0, here1 = device(me, (0, 0, 0), 0), device(me, (0, 0, 0), 1)
     is0, is1 = core_me == 0, core_me == 1
@@ -219,11 +226,23 @@
         drain(table.at[0], sib_r)
         table[0] = table[0] + sibling[...]
         pl.semaphore_wait(barrier, 2 * len(GREET) + 1)
-        for core in (0, 1):
-            send(comp.at[src], comp.at[src], cmp_s.at[core], cmp_r, device(me, PARTNER, core)).start()
-        for off in GATHER:
-            for core in (0, 1):
-                send(table.at[0], table.at[slot_of(off)], gat_s.at[core], gat_r, device(me, off, core)).start()
+
+        def positions(chips):
+            for off in chips:
+                for core in (0, 1):
+                    send(table.at[0], table.at[slot_of(off)], gat_s.at[core], gat_r, device(me, off, core)).start()
+
+        positions(GATHER[:5])
+
+        @pl.when(at_end)
+        def _():
+            for step in (1, 2):
+                far = lax.rem(z_me + jnp.where(z_low == 0, 8 - step, step), 8)
+                for core in (0, 1):
+                    to = lax.div(far, 4) * 128 + (x_me * 8 + lax.rem(far, 4) * 2 + core) * 4 + y_me
+                    send(comp.at[src], comp.at[src], cmp_s.at[core], cmp_r, to).start()
+
+        positions(GATHER[5:])
         send(table.at[0], table.at[0], gat_s.at[0], gat_r, here0).start()
 
     loads[6].wait()
@@ -231,7 +250,12 @@
     first = blk_s[0] * BLOCK_CHANNELS + lax.axis_index("ch") * CHANS
     k_mid = (NU_ZERO + (first.astype(F32) + 0.5 * (CHANS - 1)) * NU_STEP) / NU_REF
     ks = [(NU_ZERO + (first + f).astype(F32) * NU_STEP) / NU_REF for f in range(CHANS)]
-    gs = channel_factors(k_mid, 256)
+    for f, factor in enumerate(channel_factors(k_mid, 128)):
+        gs_v[f] = factor
+    choose = selectors((ROWS, 128))
+    for n, one in enumerate(choose):
+        sel_v[n] = one
+    sel_v[11] = jnp.where(one_of(rows_iota((ROWS, 128)), ODD), 1.0, 0.0)
     ant = pairs_v[...]
     chip = lax.shift_right_logical(ant, 5)
     slot = ((x_me - lax.shift_right_logical(chip, 2)) & 3) * 4 + ((z_low - chip) & 3)
@@ -242,9 +266,13 @@
     both = jnp.concatenate([comp[0], comp[1]], axis=1)
     l_row, m_row, w2_row = both[0:1, :], both[1:2, :], both[2:3, :]
     amp_row, w_row = both[3:4, :], both[4:5, :]
-    mono = monomials(l_row, m_row, w2_row, (ROWS, 512))
+    mono = monomials(l_row, m_row, w2_row, [jnp.concatenate([one] * 4, axis=1) for one in choose])
     amp_high, amp_low = split2(mono * amp_row)
     mono_amp = jnp.concatenate([amp_high, amp_low], axis=0)
+    source = jnp.broadcast_to(both[5:6, :], (128, 512))
+    rows128 = rows_iota((128, 512)).astype(F32)
+    hot_v[:, 0:512] = (source == rows128).astype(BF16)
+    hot_v[:, 512:1024] = (source + 32.0 == rows128).astype(BF16)
     cols = jnp.transpose(both)
     lcol[...] = jnp.broadcast_to(cols[:, 0:1], (512, 128))
     mcol[...] = jnp.broadcast_to(cols[:, 1:2], (512, 128))
@@ -273,24 +301,31 @@
             got.append(jnp.sum(total, axis=0, keepdims=True))
         delta_x.append(got[0])
         delta_y.append(got[1])
-    dx = jnp.concatenate(delta_x, axis=1)
-    dy = jnp.concatenate(delta_y, axis=1)
-    r2 = dx * dx + dy * dy
+    dist = [delta_x[t] * delta_x[t] + delta_y[t] * delta_y[t] for t in range(2)]
+    sel = [sel_v[n] for n in range(11)]
+    bases = [monomials(delta_x[t], delta_y[t], dist[t], sel) for t in range(2)]
 
     kx = [k_mid * d for d in delta_x]
     ky = [k_mid * d for d in delta_y]
     er = [
-        (-ENV_COEF * math.log2(math.e)) * (k_mid * k_mid) * (delta_x[t] * delta_x[t] + delta_y[t] * delta_y[t])
+        (-ENV_COEF) * (k_mid * k_mid) * dist[t]
         for t in range(2)
     ]
 
-    for i in range(32):
-        rows = slice(16 * i, 16 * i + 16)
-        lc, mc, wc = lcol[rows, :], mcol[rows, :], wcol[rows, :]
-        for t in range(2):
+    loads[7].wait()
+    loads[8].wait()
+    odd = sel_v[11] > 0.5
+    gs = [gs_v[f] for f in range(CHANS)]
+
+    eps = (ep_a, ep_b, ep_c, ep_d)
+
+    def terms(t, first, last):
+        for i in range(first, last):
+            rows = slice(16 * i, 16 * i + 16)
+            lc, mc, wc = lcol[rows, :], mcol[rows, :], wcol[rows, :]
             turns = lc * kx[t] + mc * ky[t]
-            env = jnp.exp2(wc * er[t])
-            r = turns - jnp.round(turns)
+            env = jnp.exp(wc * er[t])
+            r = turns - ((turns + ROUNDER) - ROUNDER)
             y = r * r
             s = SIN_COEFS[-1]
             for coef in SIN_COEFS[-2::-1]:
@@ -299,69 +334,82 @@
             c = COS_COEFS[-1]
             for coef in COS_COEFS[-2::-1]:
                 c = c * y + coef
-            ep_r = env * (1.0 - s * s)
-            ep_i = env * (s * c)
-            lo = 128 * t
-            high, low = split2(ep_r)
-            ep[rows, lo : lo + 128] = high
-            ep[rows, 256 + lo : 384 + lo] = low
-            high, low = split2(ep_i)
-            ep[rows, 512 + lo : 640 + lo] = high
-            ep[rows, 768 + lo : 896 + lo] = low
-
-    m_all = jnp.dot(mono_amp, ep[...], preferred_element_type=F32)
-    m_all = m_all[0:ROWS] + m_all[ROWS:]
-    m_r = m_all[:, 0:256] + m_all[:, 256:512]
-    m_i = m_all[:, 512:768] + m_all[:, 768:1024]
-    rows24 = rows_iota((ROWS, 256))
-    odd = one_of(rows24, [j for j, t in enumerate(TERMS) if (t[0] + t[1]) % 2])
-    base = monomials(dx, dy, r2, (ROWS, 256))
-    n_r = base * jnp.where(odd, m_i, m_r)
-    n_i = base * jnp.where(odd, -m_r, m_i)
-    loads[7].wait()
-    loads[8].wait()
-    zero = jnp.zeros((ROWS, 256), F32)
-    a0, d0, a1, d1, a2, d2 = zero, zero, zero, zero, zero, zero
-    resids = []
-    for f in range(CHANS):
-        v_r = jnp.sum(gs[f] * n_r, axis=0, keepdims=True)
-        v_i = jnp.sum(gs[f] * n_i, axis=0, keepdims=True)
-        rr = obs_v[0, f : f + 1, :] - v_r
-        ri = obs_v[1, f : f + 1, :] - v_i
-        resids.append((rr, ri))
-        wr = wts_v[f : f + 1, :] * rr
-        wi = wts_v[f : f + 1, :] * ri
-        k = ks[f]
-        a0 += gs[f] * wr
-        d0 += gs[f] * wi
-        a1 += gs[f] * (k * wr)
-        d1 += gs[f] * (k * wi)
-        a2 += gs[f] * (k * k * wr)
-        d2 += gs[f] * (k * k * wi)
-    resid[src] = pick(
-        rows8, [([f], resids[f][0]) for f in range(CHANS)] + [([4 + f], resids[f][1]) for f in range(CHANS)]
-    )
+            here_ep = eps[2 * t + i // 16]
+            inner_rows = slice(16 * (i % 16), 16 * (i % 16) + 16)
+            high, low = split2(env * (1.0 - s * s))
+            here_ep[inner_rows, 0:128] = high
+            here_ep[inner_rows, 256:384] = low
+            high, low = split2(env * (s * c))
+            here_ep[inner_rows, 128:256] = high
+            here_ep[inner_rows, 384:512] = low
+
+    def moments(t, h):
+        part_c = slice(256 * h, 256 * h + 256)
+        here_ep = eps[2 * t + h]
+        high = jnp.dot(mono_amp[:, part_c], here_ep[:, 0:256], preferred_element_type=F32)
+        low = jnp.dot(mono_amp[0:ROWS, part_c], here_ep[:, 256:512], preferred_element_type=F32)
+        return high[0:ROWS] + high[ROWS:] + low
+
+    def misfit(t, m_all):
+        m_r, m_i = m_all[:, 0:128], m_all[:, 128:256]
+        lanes = slice(128 * t, 128 * t + 128)
+        dx, dy, r2, base = delta_x[t], delta_y[t], dist[t], bases[t]
+        n_r = base * jnp.where(odd, m_i, m_r)
+        n_i = base * jnp.where(odd, -m_r, m_i)
+        zero = jnp.zeros((ROWS, 128), F32)
+        a0, d0, a1, d1, a2, d2 = zero, zero, zero, zero, zero, zero
+        tile = jnp.zeros((8, 128), F32)
+        rows8 = rows_iota((8, 128))
+        for f in range(CHANS):
+            v_r = jnp.sum(gs[f] * n_r, axis=0, keepdims=True)
+            v_i = jnp.sum(gs[f] * n_i, axis=0, keepdims=True)
+            rr = obs_v[0, f : f + 1, lanes] - v_r
+            ri = obs_v[1, f : f + 1, lanes] - v_i
+            tile = jnp.where(rows8 == f, rr, jnp.where(rows8 == CHANS + f, ri, tile))
+            wr = wts_v[f : f + 1, lanes] * rr
+            wi = wts_v[f : f + 1, lanes] * ri
+            k = ks[f]
+            a0 += gs[f] * wr
+            d0 += gs[f] * wi
+            a1 += gs[f] * (k * wr)
+            d1 += gs[f] * (k * wi)
+            a2 += gs[f] * (k * k * wr)
+            d2 += gs[f] * (k * k * wi)
+        resid[src, :, lanes] = tile
+
+        def sides(a, d):
+            return jnp.where(odd, -d, a) * base, jnp.where(odd, a, d) * base
+
+        c0, s0 = sides(a0, d0)
+        c1, s1 = sides(a1, d1)
+        c2, s2 = sides(a2, d2)
+        left_r = jnp.concatenate([c0, c2 * r2, -s1 * dx, -s1 * dy], axis=0)
+        left_i = jnp.concatenate([s0, s2 * r2, c1 * dx, c1 * dy], axis=0)
+        high, low = split2(jnp.concatenate([left_r, left_i], axis=1))
+        return high, jnp.concatenate([high, low], axis=0)
+
+    def adjoint(t, left_high, left_both):
+        out = []
+        for h in range(2):
+            here_ep = eps[2 * t + h]
+            high = lax.dot_general(left_both, here_ep[:, 0:256], NT, preferred_element_type=F32)
+            low = lax.dot_general(left_high, here_ep[:, 256:512], NT, preferred_element_type=F32)
+            out.append(high[0 : 4 * ROWS] + high[4 * ROWS :] + low)
+        return jnp.concatenate(out, axis=1)
+
+    terms(0, 0, 32)
+    m0 = moments(0, 0) + moments(0, 1)
+    terms(1, 0, 32)
+    m1 = moments(1, 0) + moments(1, 1)
+    left0 = misfit(0, m0)
+    y_all = adjoint(0, *left0)
+    left1 = misfit(1, m1)
     send_resid = send(
         resid.at[src], resid.at[src], res_s, res_r, jnp.where(is0, device(me, PARTNER, 0), device(me, PARTNER, 1))
     )
     send_resid.start()
-
-    def sides(a, d):
-        return jnp.where(odd, -d, a) * base, jnp.where(odd, a, d) * base
-
-    c0, s0 = sides(a0, d0)
-    c1, s1 = sides(a1, d1)
-    c2, s2 = sides(a2, d2)
-    left_r = jnp.concatenate([c0, c2 * r2, -s1 * dx, -s1 * dy], axis=0)
-    left_i = jnp.concatenate([s0, s2 * r2, c1 * dx, c1 * dy], axis=0)
-    lr = jnp.concatenate(split2(left_r), axis=0)
-    li = jnp.concatenate(split2(left_i), axis=0)
-    left = jnp.concatenate([lr, lr, li, li], axis=1)
-    y_all = lax.dot_general(left, ep[...], (((1,), (1,)), ((), ())), preferred_element_type=F32)
-    y_all = y_all[0 : 4 * ROWS] + y_all[4 * ROWS :]
-    sums = [
-        jnp.sum(y_all[q * ROWS : (q + 1) * ROWS] * mono, axis=0, keepdims=True) for q in range(4)
-    ]
+    y_all += adjoint(1, *left1)
+    sums = [jnp.sum(y_all[q * ROWS : (q + 1) * ROWS] * mono, axis=0, keepdims=True) for q in range(4)]
     norm = 1.0 / math.sqrt(16384 * BLOCK_CHANNELS)
     grads = [
         -norm * sums[0],
@@ -370,15 +418,11 @@
         (norm * 2.0 * TWO_PI * math.pi) * amp_row * w_row * sums[1],
     ]
 
-    onehot_all = (jnp.broadcast_to(both[5:6, :], (32, 512)) == rows_iota((32, 512)).astype(F32)).astype(BF16)
-    gl, gm = split3(grads[1]), split3(grads[2])
-    wide = lax.dot_general(
-        jnp.concatenate(list(gl) + list(gm), axis=0), onehot_all, (((1,), (1,)), ((), ())),
-        preferred_element_type=F32,
-    )
-    cen_l = wide[0:1, :] + wide[1:2, :] + wide[2:3, :]
-    cen_m = wide[3:4, :] + wide[4:5, :] + wide[5:6, :]
-    cen_rows = jnp.concatenate([cen_l, cen_m, jnp.zeros((1, 64), F32)], axis=1)
+    scaled = (-norm * TWO_PI) * (mono * amp_row)
+    to_l, to_m = split2(y_all[2 * ROWS : 3 * ROWS] * scaled), split2(y_all[3 * ROWS : 4 * ROWS] * scaled)
+    left = jnp.concatenate([jnp.concatenate([to_l[n], to_m[n]], axis=1) for n in range(2)], axis=0)
+    wide = lax.dot_general(left, hot_v[...], NT, preferred_element_type=F32)
+    cen_rows = jnp.sum(wide, axis=0, keepdims=True)
     for s in range(2):
         rows = rows_iota((8, 128))
         tile = 0.0
@@ -442,8 +486,11 @@
 
     @pl.when(is1)
     def _():
-        for core in (0, 1):
-            drain(comp.at[0], cmp_s.at[core])
+        @pl.when(at_end)
+        def _():
+            for core in (0, 1):
+                drain(comp, cmp_s.at[core])
+
         drain(table, gat_s.at[0])
         drain(table.at[pl.ds(1, 15)], gat_s.at[1])
         drain(recv_a.at[pl.ds(0, 7)], a_s)
@@ -495,11 +542,17 @@
             pltpu.VMEM((512, 128), F32),
             pltpu.VMEM((512, 128), F32),
             pltpu.VMEM((512, 128), F32),
-            pltpu.VMEM((512, 1024), BF16),
+            pltpu.VMEM((256, 512), BF16),
+            pltpu.VMEM((256, 512), BF16),
+            pltpu.VMEM((256, 512), BF16),
+            pltpu.VMEM((256, 512), BF16),
             pltpu.VMEM((2, 9, 128), F32),
             pltpu.VMEM((15, 9, 128), F32),
             pltpu.VMEM((16, 9, 128), F32),
             pltpu.VMEM((2, 8, 256), F32),
+            pltpu.VMEM((4, ROWS, 128), F32),
+            pltpu.VMEM((12, ROWS, 128), F32),
+            pltpu.VMEM((128, 1024), BF16),
             dma((10,)), dma(()), dma(()), dma((2,)), dma(()), dma((2,)), dma(()), dma(()), dma(()), dma(()), dma(()),
             dma((2,)), dma(()),
         ],

time: 28.2 us -> 27.7 us (0.982)
  Pallas kernels: 26.7 us -> 26.3 us
    pallas_call x1, Pallas kernels: 26.1 us -> 25.6 us  [on_device(): pl.pallas_call(kernel, out_shape=(jax.ShapeDtypeStruct((4, 256), F32), ja...]
where the time goes in v5:
time: 27.7 us; the launch traced here: 27.6 us
  Pallas kernels  26.3 us (95%)
  between operations  1.29 us (5%)
    pallas_call x1, Pallas kernels, on_device(): pl.pallas_call(kernel, out_shape=(jax.ShapeDtypeStruct((4, 256), F32), ja...  25.6 us
    pallas_call x1, Pallas kernels, on_device(): pl.pallas_call(deliver, out_shape=tuple((jax.ShapeDtypeStruct(v.shape, F3...  0.64 us

profile of v5, /device:TPU:1, one launch (start us, length us, event | category | flops | bytes accessed | tf_op | source)
XLA Modules:
  0.0 27.6 jit_solution(4906019881092297657)
XLA Ops:
  1.3 25.6 %refit.1 = (f32[4,256]{1,0:T(4,128)S(1)}, f32[2,32]{1,0:T(2,128)S(1)}, f32[2,4,512]{2,1,0:T(4,128)S(1)}) custom-call(f32[2,4,512]{2,1,0:T(4,128)} %obs_h.1, f32[4,512]{1,0:T(4,128)} %wts_h.1, s32[2,512]{1,0:T(2,128)} %pairs_h.1, f32[2,16]{1,0:T(2,128)} %bitcast.4, f32[2,32]{1,0:T(2,128)} %cen_h.1, s32[1,256]{1,0:T(1,128)} %bitcast.5, f32[1,256]{1,0:T(1,128)} %bitcast.6, ...), custom_call_target="tpu_custom_call" | custom-call | tf_op jit(solution)/shard_map/refit/pallas_call | solution.py:519
  26.9 0.6 %deliver.1 = (f32[4,256]{1,0:T(4,128)}, f32[2,32]{1,0:T(2,128)}, f32[2,4,512]{2,1,0:T(4,128)}) custom-call(f32[4,256]{1,0:T(4,128)S(1)} %get-tuple-element.6.refs_0_, f32[2,32]{1,0:T(2,128)S(1)} %get-tuple-element.7.refs_1_, f32[2,4,512]{2,1,0:T(4,128)S(1)} %get-tuple-element.8.refs_2_), custom_call_target="tpu_custom_call" | custom-call | tf_op jit(solution)/shard_map/deliver/pallas_call | solution.py:564

commit v6 on v5

--- a/solution.py
+++ b/solution.py
@@ -160,17 +160,20 @@
     obs_h, wts_h, pairs_h, pos_h, cen_h, asg_h, amp_h, off_h, wid_h, blk_h,
     comp_o, centre_o, res_o,
     obs_v, wts_v, pairs_v, pos_v, cen_v, asg_v, amp_v, off_v, wid_v, blk_s,
-    sibling, table, comp, lcol, mcol, wcol, ep_a, ep_b, ep_c, ep_d, part, recv_a, recv_b, resid, gs_v, sel_v, hot_v,
-    in_sem, sib_s, sib_r, gat_s, gat_r, cmp_s, cmp_r, res_s, res_r, a_s, a_r, b_s, b_r,
+    sibling, table, comp, lcol, mcol, wcol, ep_a, ep_b, ep_c, ep_d, part, recv_a, recv_b, resid, gs_v, sel_v, hot_v, y_v, pairs_x, obs_x, wts_x, extra,
+    in_sem, sib_s, sib_r, gat_s, gat_r, cmp_s, cmp_r, res_s, res_r, x_s, x_r, a_s, a_r, b_s, b_r,
 ):
     me = here()
     x_me, y_me, z_me, core_me = me
     src = lax.axis_index("src")
     z_low = lax.rem(z_me, 4)
-    at_end = (z_low == 0) | (z_low == 3)
     half = src * 256
     here0, here1 = device(me, (0, 0, 0), 0), device(me, (0, 0, 0), 1)
     is0, is1 = core_me == 0, core_me == 1
+    late0 = is0 & (src == 1)
+    early0 = is0 & (src == 0)
+    early1 = is1 & (src == 0)
+    at_end = (z_low == 0) | (z_low == 3)
     barrier = pltpu.get_barrier_semaphore()
     pl.semaphore_signal(barrier, 1, device_id=jnp.where(is0, here1, here0), device_id_type=LOGICAL)
     for off in GREET:
@@ -189,6 +192,14 @@
     for load in loads:
         load.start()
 
+    def hand_over():
+        third = slice(256, 384)
+        return [
+            send(pairs_h.at[:, third], pairs_x, x_s.at[0], x_r.at[0], here1),
+            send(obs_h.at[:, :, third], obs_x, x_s.at[1], x_r.at[1], here1),
+            send(wts_h.at[:, third], wts_x, x_s.at[2], x_r.at[2], here1),
+        ]
+
     loads[0].wait()
     gap = jnp.zeros((1, 16), F32)
     xs, ys = pos_v[0:1, :], pos_v[1:2, :]
@@ -199,6 +210,11 @@
         sibling[...] = jnp.concatenate([xs, gap, ys, gap, tail], axis=1)
         pl.semaphore_wait(barrier, 1)
         send(sibling, table.at[0], sib_s, sib_r, here1).start()
+
+        @pl.when(early0)
+        def _():
+            for move in hand_over():
+                move.start()
 
     @pl.when(is1)
     def _():
@@ -256,10 +272,12 @@
     for n, one in enumerate(choose):
         sel_v[n] = one
     sel_v[11] = jnp.where(one_of(rows_iota((ROWS, 128)), ODD), 1.0, 0.0)
-    ant = pairs_v[...]
-    chip = lax.shift_right_logical(ant, 5)
-    slot = ((x_me - lax.shift_right_logical(chip, 2)) & 3) * 4 + ((z_low - chip) & 3)
-    inner = ant & 31
+
+    def places(ant):
+        chip = lax.shift_right_logical(ant, 5)
+        return ((x_me - lax.shift_right_logical(chip, 2)) & 3) * 4 + ((z_low - chip) & 3), ant & 31
+
+    slot, inner = places(pairs_v[...])
     rows16 = rows_iota((16, 128))
 
     drain(comp.at[0], cmp_r)
@@ -287,44 +305,33 @@
         drain(table.at[pl.ds(1, 15)], gat_r)
 
     sites = table[:, 0, :]
-    delta_x, delta_y = [], []
-    for t in range(2):
-        lanes = slice(128 * t, 128 * t + 128)
+
+    def offsets(slot, inner):
         got = []
         for shift in (0, 32):
             total = 0.0
             for a in range(2):
-                idx = jnp.broadcast_to(inner[a : a + 1, lanes] + shift, (16, 128))
+                idx = jnp.broadcast_to(inner[a : a + 1, :] + shift, (16, 128))
                 val = jnp.take_along_axis(sites, idx, axis=1, mode="promise_in_bounds")
-                val = jnp.where(jnp.broadcast_to(slot[a : a + 1, lanes], (16, 128)) == rows16, val, 0.0)
+                val = jnp.where(jnp.broadcast_to(slot[a : a + 1, :], (16, 128)) == rows16, val, 0.0)
                 total = total + val if a == 0 else total - val
             got.append(jnp.sum(total, axis=0, keepdims=True))
-        delta_x.append(got[0])
-        delta_y.append(got[1])
-    dist = [delta_x[t] * delta_x[t] + delta_y[t] * delta_y[t] for t in range(2)]
-    sel = [sel_v[n] for n in range(11)]
-    bases = [monomials(delta_x[t], delta_y[t], dist[t], sel) for t in range(2)]
-
-    kx = [k_mid * d for d in delta_x]
-    ky = [k_mid * d for d in delta_y]
-    er = [
-        (-ENV_COEF) * (k_mid * k_mid) * dist[t]
-        for t in range(2)
-    ]
+        return got[0], got[1]
 
     loads[7].wait()
     loads[8].wait()
     odd = sel_v[11] > 0.5
     gs = [gs_v[f] for f in range(CHANS)]
+    sel = [sel_v[n] for n in range(11)]
 
     eps = (ep_a, ep_b, ep_c, ep_d)
 
-    def terms(t, first, last):
-        for i in range(first, last):
+    def terms(t, h, kx, ky, er):
+        for i in range(16 * h, 16 * h + 16):
             rows = slice(16 * i, 16 * i + 16)
             lc, mc, wc = lcol[rows, :], mcol[rows, :], wcol[rows, :]
-            turns = lc * kx[t] + mc * ky[t]
-            env = jnp.exp(wc * er[t])
+            turns = lc * kx + mc * ky
+            env = jnp.exp(wc * er)
             r = turns - ((turns + ROUNDER) - ROUNDER)
             y = r * r
             s = SIN_COEFS[-1]
@@ -350,24 +357,23 @@
         low = jnp.dot(mono_amp[0:ROWS, part_c], here_ep[:, 256:512], preferred_element_type=F32)
         return high[0:ROWS] + high[ROWS:] + low
 
-    def misfit(t, m_all):
+    def misfit(n, m_all, obs, wts, dx, dy, r2):
         m_r, m_i = m_all[:, 0:128], m_all[:, 128:256]
-        lanes = slice(128 * t, 128 * t + 128)
-        dx, dy, r2, base = delta_x[t], delta_y[t], dist[t], bases[t]
+        base = monomials(dx, dy, r2, sel)
         n_r = base * jnp.where(odd, m_i, m_r)
         n_i = base * jnp.where(odd, -m_r, m_i)
         zero = jnp.zeros((ROWS, 128), F32)
         a0, d0, a1, d1, a2, d2 = zero, zero, zero, zero, zero, zero
-        tile = jnp.zeros((8, 128), F32)
+        found = jnp.zeros((8, 128), F32)
         rows8 = rows_iota((8, 128))
         for f in range(CHANS):
             v_r = jnp.sum(gs[f] * n_r, axis=0, keepdims=True)
             v_i = jnp.sum(gs[f] * n_i, axis=0, keepdims=True)
-            rr = obs_v[0, f : f + 1, lanes] - v_r
-            ri = obs_v[1, f : f + 1, lanes] - v_i
-            tile = jnp.where(rows8 == f, rr, jnp.where(rows8 == CHANS + f, ri, tile))
-            wr = wts_v[f : f + 1, lanes] * rr
-            wi = wts_v[f : f + 1, lanes] * ri
+            rr = obs[0, f : f + 1, :] - v_r
+            ri = obs[1, f : f + 1, :] - v_i
+            found = jnp.where(rows8 == f, rr, jnp.where(rows8 == CHANS + f, ri, found))
+            wr = wts[f : f + 1, :] * rr
+            wi = wts[f : f + 1, :] * ri
             k = ks[f]
             a0 += gs[f] * wr
             d0 += gs[f] * wi
@@ -375,7 +381,7 @@
             d1 += gs[f] * (k * wi)
             a2 += gs[f] * (k * k * wr)
             d2 += gs[f] * (k * k * wi)
-        resid[src, :, lanes] = tile
+        (extra if n is None else resid.at[n])[...] = found
 
         def sides(a, d):
             return jnp.where(odd, -d, a) * base, jnp.where(odd, a, d) * base
@@ -397,18 +403,45 @@
             out.append(high[0 : 4 * ROWS] + high[4 * ROWS :] + low)
         return jnp.concatenate(out, axis=1)
 
-    terms(0, 0, 32)
-    m0 = moments(0, 0) + moments(0, 1)
-    terms(1, 0, 32)
-    m1 = moments(1, 0) + moments(1, 1)
-    left0 = misfit(0, m0)
-    y_all = adjoint(0, *left0)
-    left1 = misfit(1, m1)
-    send_resid = send(
-        resid.at[src], resid.at[src], res_s, res_r, jnp.where(is0, device(me, PARTNER, 0), device(me, PARTNER, 1))
-    )
-    send_resid.start()
-    y_all += adjoint(1, *left1)
+    def tile(n, t, slot, inner, obs, wts):
+        dx, dy = offsets(slot, inner)
+        r2 = dx * dx + dy * dy
+        scales = k_mid * dx, k_mid * dy, (-ENV_COEF * (k_mid * k_mid)) * r2
+        terms(t, 0, *scales)
+        m_all = moments(t, 0)
+        terms(t, 1, *scales)
+        m_all += moments(t, 1)
+        return adjoint(t, *misfit(n, m_all, obs, wts, dx, dy, r2))
+
+    partner = jnp.where(is0, device(me, PARTNER, 0), device(me, PARTNER, 1))
+
+    def pass_on(n, t):
+        return send(resid.at[n], resid.at[n], res_s.at[t], res_r.at[t], partner)
+
+    far, near = slice(128, 256), slice(0, 128)
+    y_v[...] = tile(2 * src + 1, 1, slot[:, far], inner[:, far], obs_v[:, :, far], wts_v[:, far])
+    pass_on(2 * src + 1, 1).start()
+
+    @pl.when(jnp.logical_not(late0))
+    def _():
+        y_v[...] += tile(2 * src, 0, slot[:, near], inner[:, near], obs_v[:, :, near], wts_v[:, near])
+        pass_on(2 * src, 0).start()
+
+    def spread():
+        return [
+            send(extra, resid.at[2], x_s.at[3], x_r.at[3], here0),
+            send(extra, resid.at[2], x_s.at[4], x_r.at[3], device(me, PARTNER, 0)),
+        ]
+
+    @pl.when(early1)
+    def _():
+        for n, ref in enumerate((pairs_x, obs_x, wts_x)):
+            drain(ref, x_r.at[n])
+        y_v[...] += tile(None, 0, *places(pairs_x[...]), obs_x, wts_x)
+        for move in spread():
+            move.start()
+
+    y_all = y_v[...]
     sums = [jnp.sum(y_all[q * ROWS : (q + 1) * ROWS] * mono, axis=0, keepdims=True) for q in range(4)]
     norm = 1.0 / math.sqrt(16384 * BLOCK_CHANNELS)
     grads = [
@@ -425,12 +458,12 @@
     cen_rows = jnp.sum(wide, axis=0, keepdims=True)
     for s in range(2):
         rows = rows_iota((8, 128))
-        tile = 0.0
+        block = 0.0
         for h in range(2):
             lo = 256 * s + 128 * h
             for q in range(4):
-                tile = jnp.where(rows == 4 * h + q, grads[q][:, lo : lo + 128], tile)
-        part[s, 0:8, :] = tile
+                block = jnp.where(rows == 4 * h + q, grads[q][:, lo : lo + 128], block)
+        part[s, 0:8, :] = block
         part[s, 8:9, :] = cen_rows
 
     def column(core):
@@ -451,15 +484,24 @@
         for i in range(15):
             total = total + recv_a[i]
         recv_b[0] = total
-        for i, off in enumerate(PLANE):
-            for core in (0, 1):
+        for core in (1, 0):
+            for i, off in enumerate(PLANE):
                 send(recv_b.at[0], recv_b.at[i + 1], b_s.at[core], b_r, device(me, off, core)).start()
         send(recv_b.at[0], recv_b.at[0], b_s.at[0], b_r, here0).start()
 
-    send_resid.wait_recv()
-    for h in range(2):
-        res_o[0, :, 256 * h : 256 * h + 256] = resid[h, 0:4, :]
-        res_o[1, :, 256 * h : 256 * h + 256] = resid[h, 4:8, :]
+    drain(resid.at[0], res_r.at[1])
+
+    @pl.when(jnp.logical_not(early0))
+    def _():
+        drain(resid.at[0], res_r.at[0])
+
+    @pl.when(is0)
+    def _():
+        drain(extra, x_r.at[3])
+
+    for n in range(4):
+        res_o[0, :, 128 * n : 128 * n + 128] = resid[n, 0:4, :]
+        res_o[1, :, 128 * n : 128 * n + 128] = resid[n, 4:8, :]
 
     @pl.when(is0)
     def _():
@@ -477,7 +519,21 @@
     centre_o[0:1, :] = total[8:9, 0:32]
     centre_o[1:2, :] = total[8:9, 32:64]
 
-    send_resid.wait_send()
+    drain(resid.at[0], res_s.at[1])
+
+    @pl.when(jnp.logical_not(late0))
+    def _():
+        drain(resid.at[0], res_s.at[0])
+
+    @pl.when(early0)
+    def _():
+        for move in hand_over():
+            move.wait_send()
+
+    @pl.when(early1)
+    def _():
+        for move in spread():
+            move.wait_send()
 
     @pl.when(is0)
     def _():
@@ -549,11 +605,16 @@
             pltpu.VMEM((2, 9, 128), F32),
             pltpu.VMEM((15, 9, 128), F32),
             pltpu.VMEM((16, 9, 128), F32),
-            pltpu.VMEM((2, 8, 256), F32),
+            pltpu.VMEM((4, 8, 128), F32),
             pltpu.VMEM((4, ROWS, 128), F32),
             pltpu.VMEM((12, ROWS, 128), F32),
             pltpu.VMEM((128, 1024), BF16),
-            dma((10,)), dma(()), dma(()), dma((2,)), dma(()), dma((2,)), dma(()), dma(()), dma(()), dma(()), dma(()),
+            pltpu.VMEM((4 * ROWS, 512), F32),
+            pltpu.VMEM((2, 128), jnp.int32),
+            pltpu.VMEM((2, 4, 128), F32),
+            pltpu.VMEM((4, 128), F32),
+            pltpu.VMEM((8, 128), F32),
+            dma((10,)), dma(()), dma(()), dma((2,)), dma(()), dma((2,)), dma(()), dma((2,)), dma((2,)), dma((5,)), dma((4,)), dma(()), dma(()),
             dma((2,)), dma(()),
         ],
         compiler_params=pltpu.CompilerParams(

time: 27.7 us -> 27.1 us (0.978)
  Pallas kernels: 26.3 us -> 25.7 us
    pallas_call x1, Pallas kernels: 25.6 us -> 25 us  [on_device(): pl.pallas_call(kernel, out_shape=(jax.ShapeDtypeStruct((4, 256), F32), ja...]
where the time goes in v6:
time: 27.1 us; the launch traced here: 26.9 us
  Pallas kernels  25.7 us (95%)
  between operations  1.29 us (5%)
    pallas_call x1, Pallas kernels, on_device(): pl.pallas_call(kernel, out_shape=(jax.ShapeDtypeStruct((4, 256), F32), ja...  25 us
    pallas_call x1, Pallas kernels, on_device(): pl.pallas_call(deliver, out_shape=tuple((jax.ShapeDtypeStruct(v.shape, F3...  0.64 us

profile of v6, /device:TPU:1, one launch (start us, length us, event | category | flops | bytes accessed | tf_op | source)
XLA Modules:
  0.0 26.9 jit_solution(4377421131538279593)
XLA Ops:
  1.3 25.0 %refit.1 = (f32[4,256]{1,0:T(4,128)S(1)}, f32[2,32]{1,0:T(2,128)S(1)}, f32[2,4,512]{2,1,0:T(4,128)S(1)}) custom-call(f32[2,4,512]{2,1,0:T(4,128)} %obs_h.1, f32[4,512]{1,0:T(4,128)} %wts_h.1, s32[2,512]{1,0:T(2,128)} %pairs_h.1, f32[2,16]{1,0:T(2,128)} %bitcast.4, f32[2,32]{1,0:T(2,128)} %cen_h.1, s32[1,256]{1,0:T(1,128)} %bitcast.5, f32[1,256]{1,0:T(1,128)} %bitcast.6, ...), custom_call_target="tpu_custom_call" | custom-call | tf_op jit(solution)/shard_map/refit/pallas_call | solution.py:575
  26.3 0.6 %deliver.1 = (f32[4,256]{1,0:T(4,128)}, f32[2,32]{1,0:T(2,128)}, f32[2,4,512]{2,1,0:T(4,128)}) custom-call(f32[4,256]{1,0:T(4,128)S(1)} %get-tuple-element.6.refs_0_, f32[2,32]{1,0:T(2,128)S(1)} %get-tuple-element.7.refs_1_, f32[2,4,512]{2,1,0:T(4,128)S(1)} %get-tuple-element.8.refs_2_), custom_call_target="tpu_custom_call" | custom-call | tf_op jit(solution)/shard_map/deliver/pallas_call | solution.py:625

commit v7 on v6

--- a/solution.py
+++ b/solution.py
@@ -159,9 +159,9 @@
 def kernel(
     obs_h, wts_h, pairs_h, pos_h, cen_h, asg_h, amp_h, off_h, wid_h, blk_h,
     comp_o, centre_o, res_o,
-    obs_v, wts_v, pairs_v, pos_v, cen_v, asg_v, amp_v, off_v, wid_v, blk_s,
+    obs_v, wts_v, pairs_v, pos_v, cen_v, asg_v, amp_v, off_v, wid_v, blk_s, row_s,
     sibling, table, comp, lcol, mcol, wcol, ep_a, ep_b, ep_c, ep_d, part, recv_a, recv_b, resid, gs_v, sel_v, hot_v, y_v, pairs_x, obs_x, wts_x, extra,
-    in_sem, sib_s, sib_r, gat_s, gat_r, cmp_s, cmp_r, res_s, res_r, x_s, x_r, a_s, a_r, b_s, b_r,
+    in_sem, row_sem, sib_s, sib_r, gat_s, gat_r, cmp_s, cmp_r, res_s, res_r, x_s, x_r, a_s, a_r, b_s, b_r,
 ):
     me = here()
     x_me, y_me, z_me, core_me = me
@@ -241,12 +241,15 @@
     def _():
         drain(table.at[0], sib_r)
         table[0] = table[0] + sibling[...]
+        to_scalar = pltpu.make_async_copy(table.at[0], row_s, row_sem)
+        to_scalar.start()
+        to_scalar.wait()
         pl.semaphore_wait(barrier, 2 * len(GREET) + 1)
 
         def positions(chips):
             for off in chips:
                 for core in (0, 1):
-                    send(table.at[0], table.at[slot_of(off)], gat_s.at[core], gat_r, device(me, off, core)).start()
+                    send(row_s, table.at[slot_of(off)], gat_s.at[core], gat_r, device(me, off, core)).start()
 
         positions(GATHER[:5])
 
@@ -259,7 +262,7 @@
                     send(comp.at[src], comp.at[src], cmp_s.at[core], cmp_r, to).start()
 
         positions(GATHER[5:])
-        send(table.at[0], table.at[0], gat_s.at[0], gat_r, here0).start()
+        send(row_s, table.at[0], gat_s.at[0], gat_r, here0).start()
 
     loads[6].wait()
     loads[9].wait()
@@ -287,10 +290,9 @@
     mono = monomials(l_row, m_row, w2_row, [jnp.concatenate([one] * 4, axis=1) for one in choose])
     amp_high, amp_low = split2(mono * amp_row)
     mono_amp = jnp.concatenate([amp_high, amp_low], axis=0)
+    rows128 = rows_iota((128, 512))
     source = jnp.broadcast_to(both[5:6, :], (128, 512))
-    rows128 = rows_iota((128, 512)).astype(F32)
-    hot_v[:, 0:512] = (source == rows128).astype(BF16)
-    hot_v[:, 512:1024] = (source + 32.0 == rows128).astype(BF16)
+    hot_v[...] = ((source == (rows128 & 31).astype(F32)) & (rows128 < 64)).astype(BF16)
     cols = jnp.transpose(both)
     lcol[...] = jnp.broadcast_to(cols[:, 0:1], (512, 128))
     mcol[...] = jnp.broadcast_to(cols[:, 1:2], (512, 128))
@@ -343,10 +345,11 @@
                 c = c * y + coef
             here_ep = eps[2 * t + i // 16]
             inner_rows = slice(16 * (i % 16), 16 * (i % 16) + 16)
-            high, low = split2(env * (1.0 - s * s))
+            es = env * s
+            high, low = split2(env - es * s)
             here_ep[inner_rows, 0:128] = high
             here_ep[inner_rows, 256:384] = low
-            high, low = split2(env * (s * c))
+            high, low = split2(es * c)
             here_ep[inner_rows, 128:256] = high
             here_ep[inner_rows, 384:512] = low
 
@@ -451,11 +454,16 @@
         (norm * 2.0 * TWO_PI * math.pi) * amp_row * w_row * sums[1],
     ]
 
-    scaled = (-norm * TWO_PI) * (mono * amp_row)
-    to_l, to_m = split2(y_all[2 * ROWS : 3 * ROWS] * scaled), split2(y_all[3 * ROWS : 4 * ROWS] * scaled)
-    left = jnp.concatenate([jnp.concatenate([to_l[n], to_m[n]], axis=1) for n in range(2)], axis=0)
+    rows8w = rows_iota((8, 512))
+    pair = jnp.where(rows8w < 2, grads[1], grads[2])
+    high = pair * 65537.0
+    high = high - (high - pair)
+    left = jnp.where((rows8w & 1) == 0, high, pair - high).astype(BF16)
     wide = lax.dot_general(left, hot_v[...], NT, preferred_element_type=F32)
-    cen_rows = jnp.sum(wide, axis=0, keepdims=True)
+    lanes1 = lax.broadcasted_iota(jnp.int32, (8, 128), 1)
+    rows8n = rows_iota((8, 128))
+    mine = (rows8n < 4) & (lax.shift_right_logical(rows8n, 1) == lax.shift_right_logical(lanes1, 5))
+    cen_rows = jnp.sum(jnp.where(mine, wide, 0.0), axis=0, keepdims=True)
     for s in range(2):
         rows = rows_iota((8, 128))
         block = 0.0
@@ -592,6 +600,7 @@
             pltpu.VMEM((2, 256), F32),
             pltpu.VMEM((1, 256), F32),
             pltpu.SMEM((1,), jnp.int32),
+            pltpu.SMEM((1, 128), F32),
             pltpu.VMEM((1, 128), F32),
             pltpu.VMEM((16, 1, 128), F32),
             pltpu.VMEM((2, 8, 256), F32),
@@ -608,13 +617,13 @@
             pltpu.VMEM((4, 8, 128), F32),
             pltpu.VMEM((4, ROWS, 128), F32),
             pltpu.VMEM((12, ROWS, 128), F32),
-            pltpu.VMEM((128, 1024), BF16),
+            pltpu.VMEM((128, 512), BF16),
             pltpu.VMEM((4 * ROWS, 512), F32),
             pltpu.VMEM((2, 128), jnp.int32),
             pltpu.VMEM((2, 4, 128), F32),
             pltpu.VMEM((4, 128), F32),
             pltpu.VMEM((8, 128), F32),
-            dma((10,)), dma(()), dma(()), dma((2,)), dma(()), dma((2,)), dma(()), dma((2,)), dma((2,)), dma((5,)), dma((4,)), dma(()), dma(()),
+            dma((10,)), dma(()), dma(()), dma(()), dma((2,)), dma(()), dma((2,)), dma(()), dma((2,)), dma((2,)), dma((5,)), dma((4,)), dma(()), dma(()),
             dma((2,)), dma(()),
         ],
         compiler_params=pltpu.CompilerParams(

time: 27.1 us -> 26.9 us (level)
  no operation moved by 1% of the time
where the time goes in v7:
time: 26.9 us; the launch traced here: 26.8 us
  Pallas kernels  25.5 us (95%)
  between operations  1.29 us (5%)
    pallas_call x1, Pallas kernels, on_device(): pl.pallas_call(kernel, out_shape=(jax.ShapeDtypeStruct((4, 256), F32), ja...  24.8 us
    pallas_call x1, Pallas kernels, on_device(): pl.pallas_call(deliver, out_shape=tuple((jax.ShapeDtypeStruct(v.shape, F3...  0.64 us

profile of v7, /device:TPU:1, one launch (start us, length us, event | category | flops | bytes accessed | tf_op | source)
XLA Modules:
  0.0 26.8 jit_solution(8444382620351499512)
XLA Ops:
  1.3 24.8 %refit.1 = (f32[4,256]{1,0:T(4,128)S(1)}, f32[2,32]{1,0:T(2,128)S(1)}, f32[2,4,512]{2,1,0:T(4,128)S(1)}) custom-call(f32[2,4,512]{2,1,0:T(4,128)} %obs_h.1, f32[4,512]{1,0:T(4,128)} %wts_h.1, s32[2,512]{1,0:T(2,128)} %pairs_h.1, f32[2,16]{1,0:T(2,128)} %bitcast.4, f32[2,32]{1,0:T(2,128)} %cen_h.1, s32[1,256]{1,0:T(1,128)} %bitcast.5, f32[1,256]{1,0:T(1,128)} %bitcast.6, ...), custom_call_target="tpu_custom_call" | custom-call | tf_op jit(solution)/shard_map/refit/pallas_call | solution.py:583
  26.1 0.6 %deliver.1 = (f32[4,256]{1,0:T(4,128)}, f32[2,32]{1,0:T(2,128)}, f32[2,4,512]{2,1,0:T(4,128)}) custom-call(f32[4,256]{1,0:T(4,128)S(1)} %get-tuple-element.6.refs_0_, f32[2,32]{1,0:T(2,128)S(1)} %get-tuple-element.7.refs_1_, f32[2,4,512]{2,1,0:T(4,128)S(1)} %get-tuple-element.8.refs_2_), custom_call_target="tpu_custom_call" | custom-call | tf_op jit(solution)/shard_map/deliver/pallas_call | solution.py:634

commit v8 on v7

--- a/solution.py
+++ b/solution.py
@@ -289,7 +289,7 @@
     amp_row, w_row = both[3:4, :], both[4:5, :]
     mono = monomials(l_row, m_row, w2_row, [jnp.concatenate([one] * 4, axis=1) for one in choose])
     amp_high, amp_low = split2(mono * amp_row)
-    mono_amp = jnp.concatenate([amp_high, amp_low], axis=0)
+    mono_amp = jnp.concatenate([amp_high.astype(F32), amp_low.astype(F32)], axis=0).astype(BF16)
     rows128 = rows_iota((128, 512))
     source = jnp.broadcast_to(both[5:6, :], (128, 512))
     hot_v[...] = ((source == (rows128 & 31).astype(F32)) & (rows128 < 64)).astype(BF16)
@@ -357,7 +357,7 @@
         part_c = slice(256 * h, 256 * h + 256)
         here_ep = eps[2 * t + h]
         high = jnp.dot(mono_amp[:, part_c], here_ep[:, 0:256], preferred_element_type=F32)
-        low = jnp.dot(mono_amp[0:ROWS, part_c], here_ep[:, 256:512], preferred_element_type=F32)
+        low = jnp.dot(amp_high[:, part_c], here_ep[:, 256:512], preferred_element_type=F32)
         return high[0:ROWS] + high[ROWS:] + low
 
     def misfit(n, m_all, obs, wts, dx, dy, r2):

time: 26.9 us -> 26.9 us (level)
  no operation moved by 1% of the time
where the time goes in v8:
time: 26.9 us; the launch traced here: 26.8 us
  Pallas kernels  25.5 us (95%)
  between operations  1.29 us (5%)
    pallas_call x1, Pallas kernels, on_device(): pl.pallas_call(kernel, out_shape=(jax.ShapeDtypeStruct((4, 256), F32), ja...  24.8 us
    pallas_call x1, Pallas kernels, on_device(): pl.pallas_call(deliver, out_shape=tuple((jax.ShapeDtypeStruct(v.shape, F3...  0.64 us

profile of v8, /device:TPU:1, one launch (start us, length us, event | category | flops | bytes accessed | tf_op | source)
XLA Modules:
  0.0 26.8 jit_solution(16483873883247525587)
XLA Ops:
  1.3 24.8 %refit.1 = (f32[4,256]{1,0:T(4,128)S(1)}, f32[2,32]{1,0:T(2,128)S(1)}, f32[2,4,512]{2,1,0:T(4,128)S(1)}) custom-call(f32[2,4,512]{2,1,0:T(4,128)} %obs_h.1, f32[4,512]{1,0:T(4,128)} %wts_h.1, s32[2,512]{1,0:T(2,128)} %pairs_h.1, f32[2,16]{1,0:T(2,128)} %bitcast.4, f32[2,32]{1,0:T(2,128)} %cen_h.1, s32[1,256]{1,0:T(1,128)} %bitcast.5, f32[1,256]{1,0:T(1,128)} %bitcast.6, ...), custom_call_target="tpu_custom_call" | custom-call | tf_op jit(solution)/shard_map/refit/pallas_call | solution.py:583
  26.1 0.6 %deliver.1 = (f32[4,256]{1,0:T(4,128)}, f32[2,32]{1,0:T(2,128)}, f32[2,4,512]{2,1,0:T(4,128)}) custom-call(f32[4,256]{1,0:T(4,128)S(1)} %get-tuple-element.6.refs_0_, f32[2,32]{1,0:T(2,128)S(1)} %get-tuple-element.7.refs_1_, f32[2,4,512]{2,1,0:T(4,128)S(1)} %get-tuple-element.8.refs_2_), custom_call_target="tpu_custom_call" | custom-call | tf_op jit(solution)/shard_map/deliver/pallas_call | solution.py:634

commit v9 on v8

--- a/solution.py
+++ b/solution.py
@@ -474,19 +474,20 @@
         part[s, 0:8, :] = block
         part[s, 8:9, :] = cen_rows
 
-    def column(core):
-        for i, off in enumerate(COLUMN):
-            to = lax.div(lax.rem(z_me + (off[2] + 8), 8), 4)
-            send(part.at[to], recv_a.at[2 * i + core], a_s, a_r, device(me, off, 1)).start()
+        for low in range(4):
+            @pl.when(z_me != 4 * s + low)
+            def _(s=s, low=low):
+                back = lax.rem(4 * s + low + 8 - z_me, 8) - 1
+                to = s * 128 + (x_me * 8 + low * 2 + 1) * 4 + y_me
+                send(part.at[s], recv_a.at[2 * back + core_me], a_s, a_r, to).start()
+
 
     @pl.when(is0)
     def _():
-        column(0)
         send(part.at[src], recv_a.at[14], a_s, a_r, here1).start()
 
     @pl.when(is1)
     def _():
-        column(1)
         drain(recv_a, a_r)
         total = part[src]
         for i in range(15):

time: 26.9 us -> 26.7 us (level)
  Pallas kernels: 25.5 us -> 25.2 us
where the time goes in v9:
time: 26.7 us; the launch traced here: 26.5 us
  Pallas kernels  25.2 us (94%)
  between operations  1.29 us (5%)
    pallas_call x1, Pallas kernels, on_device(): pl.pallas_call(kernel, out_shape=(jax.ShapeDtypeStruct((4, 256), F32), ja...  24.6 us
    pallas_call x1, Pallas kernels, on_device(): pl.pallas_call(deliver, out_shape=tuple((jax.ShapeDtypeStruct(v.shape, F3...  0.64 us

profile of v9, /device:TPU:1, one launch (start us, length us, event | category | flops | bytes accessed | tf_op | source)
XLA Modules:
  0.0 26.5 jit_solution(12063912907412315466)
XLA Ops:
  1.3 24.6 %refit.1 = (f32[4,256]{1,0:T(4,128)S(1)}, f32[2,32]{1,0:T(2,128)S(1)}, f32[2,4,512]{2,1,0:T(4,128)S(1)}) custom-call(f32[2,4,512]{2,1,0:T(4,128)} %obs_h.1, f32[4,512]{1,0:T(4,128)} %wts_h.1, s32[2,512]{1,0:T(2,128)} %pairs_h.1, f32[2,16]{1,0:T(2,128)} %bitcast.4, f32[2,32]{1,0:T(2,128)} %cen_h.1, s32[1,256]{1,0:T(1,128)} %bitcast.5, f32[1,256]{1,0:T(1,128)} %bitcast.6, ...), custom_call_target="tpu_custom_call" | custom-call | tf_op jit(solution)/shard_map/refit/pallas_call | solution.py:584
  25.9 0.6 %deliver.1 = (f32[4,256]{1,0:T(4,128)}, f32[2,32]{1,0:T(2,128)}, f32[2,4,512]{2,1,0:T(4,128)}) custom-call(f32[4,256]{1,0:T(4,128)S(1)} %get-tuple-element.6.refs_0_, f32[2,32]{1,0:T(2,128)S(1)} %get-tuple-element.7.refs_1_, f32[2,4,512]{2,1,0:T(4,128)S(1)} %get-tuple-element.8.refs_2_), custom_call_target="tpu_custom_call" | custom-call | tf_op jit(solution)/shard_map/deliver/pallas_call | solution.py:635
